TPU v7x, 128 devices: a whole 4x4x4 slice. The times are simulated.
128 devices in a mesh: seq: 8 (over y, z_lo), head: 16 (over z_hi, x, core).
Axes of the slice: x: 4, y: 4, z: 4 (z_hi: 2, z_lo: 2; z = z_hi * 2 + z_lo), core: 2. Of those that a mesh axis runs over, the one named last changes fastest.
Arguments:
- inner_x: bfloat16 [8192, 16384], P('seq', 'head'), may hold values from -6 to 6
- gate_z: bfloat16 [8192, 16384], P('seq', 'head'), may hold values from -6 to 6
- dt_raw: bfloat16 [256, 8192], P('head', 'seq'), may hold values from -4.7 to 4.7
- b_proj: bfloat16 [8192, 2048], P(('seq', 'head')), may hold values from -3 to 3
- c_proj: bfloat16 [8192, 2048], P(('seq', 'head')), may hold values from -0.375 to 0.375
- a_log: float32 [256], P('head'), may hold values from -12 to 0
- dt_bias: float32 [256], P('head'), may hold values from -4 to -3
- d_skip: float32 [256], P('head'), may hold values from 0.5 to 2
- grad_gated: bfloat16 [8192, 16384], P('seq', 'head'), may hold values from -16 to 16
Outputs:
- gated: bfloat16 [8192, 16384], P('seq', 'head')
- grad_x: bfloat16 [8192, 16384], P('seq', 'head')
- grad_z: bfloat16 [8192, 16384], P('seq', 'head')
- grad_dt: bfloat16 [256, 8192], P('head', 'seq')
- grad_b: bfloat16 [8192, 2048], P(('seq', 'head'))
- grad_c: bfloat16 [8192, 2048], P(('seq', 'head'))
- grad_alog: float32 [256], P('head')
- grad_bias: float32 [256], P('head')
- grad_skip: float32 [256], P('head')
All inputs are finite; a program needn't handle non-finite values.
Results may differ from a plain program's by a relative error of at most 0.014.
Values may be sent and summed in bfloat16 or wider, within the bound.
A program may use at most 256 MiB of HBM per device.

v0:
```python
import jax
import jax.numpy as jnp
from jax import lax
from jax.sharding import PartitionSpec as P

HEAD_DIM = 64
STATE = 256
GROUPS = 8
STRETCH = 128


highest = lax.Precision.HIGHEST


def prefix(value, axis, join, neutral, backward):
    count = lax.axis_size(axis)
    place = lax.axis_index(axis)
    ahead = count - 1 - place if backward else place
    gathered = jax.tree.map(
        lambda a, kind: lax.all_gather(a.astype(kind), axis), value, (jnp.bfloat16, jnp.bfloat16)
    )
    state = jax.tree.map(lambda a, e: jnp.zeros_like(a) + jnp.asarray(e, a.dtype), value, neutral)

    def one(lap, state):
        source = count - 1 - lap if backward else lap
        return join(
            state,
            jax.tree.map(
                lambda a, own: lax.dynamic_index_in_dim(a, source, 0, False).astype(own.dtype),
                gathered,
                value,
            ),
        )

    return lax.fori_loop(0, ahead, one, state)


def stretch_scan(values, steps, decays, b_rows, c_rows, start_state):
    cum_decay = jnp.cumsum(decays, axis=2)
    positions = jnp.arange(values.shape[1])
    lower_mask = positions[:, None] >= positions[None, :]
    segments = cum_decay[:, :, :, None] - cum_decay[:, :, None, :]
    decay_mask = jnp.exp(jnp.where(lower_mask, segments, -jnp.inf))
    scores = jnp.einsum("cin,cjn->cij", c_rows, b_rows, precision=highest)
    mixing = scores[None] * decay_mask * steps[:, :, None, :]
    y_diag = jnp.einsum("kcij,cjkp->cikp", mixing, values, precision=highest)
    last_decay = cum_decay[:, :, -1:]
    weights = jnp.exp(last_decay - cum_decay) * steps
    scaled = values * jnp.transpose(weights, (1, 2, 0))[..., None]
    states = jnp.einsum("cjn,cjkp->cknp", b_rows, scaled, precision=highest)
    totals = jnp.transpose(last_decay[:, :, 0])

    def advance(state_now, inputs):
        total_step, local_state = inputs
        return (jnp.exp(total_step)[:, None, None] * state_now + local_state, state_now)

    final_state, starts = lax.scan(advance, start_state, (totals, states))
    y_off = jnp.einsum("cin,cknp->cikp", c_rows, starts, precision=highest)
    y_off = y_off * jnp.transpose(jnp.exp(cum_decay), (1, 2, 0))[..., None]
    return (y_diag + y_off, final_state)


def mixer_local(inner_x, gate_z, dt_raw, b_group, c_group, a_log, dt_bias, d_skip, start_state):
    token_count = inner_x.shape[0]
    head_count = a_log.shape[0]
    blocks = token_count // STRETCH
    step_size = jax.nn.softplus(dt_raw.astype(jnp.float32) + dt_bias[:, None])
    log_decay = -jnp.exp(a_log)[:, None] * step_size
    values = inner_x.astype(jnp.float32).reshape(blocks, STRETCH, head_count, HEAD_DIM)
    y_core, final_state = stretch_scan(
        values,
        step_size.reshape(head_count, blocks, STRETCH),
        log_decay.reshape(head_count, blocks, STRETCH),
        b_group.reshape(blocks, STRETCH, STATE),
        c_group.reshape(blocks, STRETCH, STATE),
        start_state,
    )
    y_full = y_core + d_skip[None, None, :, None] * values
    y_full = y_full.reshape(token_count, head_count * HEAD_DIM)
    return (y_full * jax.nn.silu(gate_z.astype(jnp.float32)), final_state)


def link_states(earlier, later):
    decay_early, state_early = earlier
    decay_late, state_late = later
    return (decay_early + decay_late, jnp.exp(decay_late)[:, None, None] * state_early + state_late)


def widen_group(part, group_index):
    blank = jnp.zeros((part.shape[0], GROUPS * STATE), jnp.float32)
    return lax.dynamic_update_slice_in_dim(blank, part, group_index * STATE, 1)


def per_device(inner_x, gate_z, dt_raw, b_proj, c_proj, a_log, dt_bias, d_skip, grad_gated):
    token_count = inner_x.shape[0]
    head_count = a_log.shape[0]
    group_span = lax.axis_size("head") // GROUPS
    group_index = lax.axis_index("head") // group_span
    full_b, full_c = (
        lax.all_gather(b_proj, "head", axis=0, tiled=True),
        lax.all_gather(c_proj, "head", axis=0, tiled=True),
    )
    b_group = lax.dynamic_slice_in_dim(full_b, group_index * STATE, STATE, 1)
    c_group = lax.dynamic_slice_in_dim(full_c, group_index * STATE, STATE, 1)
    b_float = b_group.astype(jnp.float32)
    c_float = c_group.astype(jnp.float32)
    step_size = jax.nn.softplus(dt_raw.astype(jnp.float32) + dt_bias[:, None])
    log_decay = -jnp.exp(a_log)[:, None] * step_size
    cum_decay = jnp.cumsum(log_decay, axis=1)
    decay_total = cum_decay[:, -1]
    values = inner_x.astype(jnp.float32).reshape(token_count, head_count, HEAD_DIM)
    weights = jnp.exp(decay_total[:, None] - cum_decay) * step_size
    state_local = jnp.einsum(
        "tn,tkp->knp", b_float, values * jnp.transpose(weights)[:, :, None], precision=highest
    )
    grad_float = grad_gated.astype(jnp.float32)
    grad_y = (grad_float * jax.nn.silu(gate_z.astype(jnp.float32))).reshape(
        token_count, head_count, HEAD_DIM
    )
    adjoint_local = jnp.einsum(
        "tn,tkp->knp",
        c_float,
        grad_y * jnp.transpose(jnp.exp(cum_decay))[:, :, None],
        precision=highest,
    )
    identity = (jnp.zeros((head_count,), jnp.float32), jnp.zeros_like(state_local))
    start_state = prefix((decay_total, state_local), "seq", link_states, identity, False)[1]
    end_adjoint = prefix((decay_total, adjoint_local), "seq", link_states, identity, True)[1]

    def local_mixer(x_in, z_in, dt_in, b_in, c_in, alog_in, bias_in, skip_in):
        return mixer_local(x_in, z_in, dt_in, b_in, c_in, alog_in, bias_in, skip_in, start_state)

    primal, pullback = jax.vjp(
        local_mixer, inner_x, gate_z, dt_raw, b_float, c_float, a_log, dt_bias, d_skip
    )
    gated_value = primal[0]
    grads = pullback((grad_float, end_adjoint))
    grad_alog, grad_bias, grad_skip = lax.psum((grads[5], grads[6], grads[7]), "seq")
    summed_b, summed_c = (
        lax.psum_scatter(
            widen_group(grads[3], group_index).astype(jnp.bfloat16),
            "head",
            scatter_dimension=0,
            tiled=True,
        ).astype(jnp.float32),
        lax.psum_scatter(
            widen_group(grads[4], group_index).astype(jnp.bfloat16),
            "head",
            scatter_dimension=0,
            tiled=True,
        ).astype(jnp.float32),
    )
    return (
        gated_value.astype(jnp.bfloat16),
        grads[0],
        grads[1],
        grads[2],
        summed_b.astype(jnp.bfloat16),
        summed_c.astype(jnp.bfloat16),
        grad_alog,
        grad_bias,
        grad_skip,
    )


def solution(mesh):
    in_specs = (
        P("seq", "head"),
        P("seq", "head"),
        P("head", "seq"),
        P(("seq", "head"), None),
        P(("seq", "head"), None),
        P("head"),
        P("head"),
        P("head"),
        P("seq", "head"),
    )
    out_specs = (
        P("seq", "head"),
        P("seq", "head"),
        P("seq", "head"),
        P("head", "seq"),
        P(("seq", "head"), None),
        P(("seq", "head"), None),
        P("head"),
        P("head"),
        P("head"),
    )
    return jax.shard_map(
        per_device, mesh=mesh, in_specs=in_specs, out_specs=out_specs, check_vma=False
    )
```

profile of v0, /device:TPU:32, one launch (start us, length us, event | category | flops | bytes accessed | tf_op | source)
XLA Modules:
  0.0 672.2 jit_solution(16996236171857211974)
XLA Ops:
  10.3 4.5 reduce_window_sum.36
  19.1 48.6 %all-gather.10.cloned.1.call-done = bf16[1024,2048]{1,0:T(8,128)(2,1)} async-done(((bf16[64,2048]{1,0:T(8,128)(2,1)}), bf16[1024,2048]{1,0:T(8,128)(2,1)}) %all-gather.10.cloned.1.call-update) | async-done | bytes 4194320 | tf_op jit(solution)/shard_map/all_gather | solution.py:100
  73.7 17.5 %all-reduce.1 = bf16[128]{0:T(256)(128)(2,1)S(1)} all-reduce(bf16[128]{0:T(256)(128)(2,1)S(1)} %dynamic-update-slice), channel_id=2, replica_groups=mesh['seq'=8,'head'=16] {'seq'}, use_global_device_ids=true, to_apply=%add.1 | all-reduce | flops 128 | bytes 512
  93.2 3.9 copy.138
  97.2 3.9 copy.139
  104.6 20.4 %all-gather.8.cloned.1.call-done = bf16[1024,2048]{1,0:T(8,128)(2,1)} async-done(((bf16[64,2048]{1,0:T(8,128)(2,1)}), bf16[1024,2048]{1,0:T(8,128)(2,1)}) %all-gather.8.cloned.1.call-update) | async-done | bytes 4194320 | tf_op jit(solution)/shard_map/all_gather | solution.py:101
  128.0 9.0 %fusion.56 = f32[8,16,256,64]{2,3,1,0:T(8,128)} fusion(bf16[8,128,256,1]{2,1,3,0:T(8,128)(2,1)S(1)} %bitcast.257, f32[8,128,16,64]{1,0,3,2:T(8,128)} %bitcast.237, f32[8,128,16]{1,2,0:T(8,128)S(1)} %copy.131), kind=kOutput, calls=%fused_computation.88 | convolution fusion | flops 3222274048 | bytes 13172736 | tf_op jit(solution)/shard_map/jvp(cjn,cjkp->cknp)/dot_general | solution.py:50
  137.0 77.7 %all-gather.12.cloned.1.call-done = bf16[128,256,64]{1,2,0:T(8,128)(2,1)} async-done(((bf16[16,256,64]{1,2,0:T(8,128)(2,1)}), bf16[128,256,64]{1,2,0:T(8,128)(2,1)}) %all-gather.12.cloned.1.call-update) | async-done | bytes 4194320 | tf_op jit(solution)/shard_map/all_gather | solution.py:20
  214.9 4.3 while.60
  219.3 7.9 %broadcast.36.clone = f32[8,16,256,64]{3,2,1,0:T(8,128)} broadcast(f32[]{:T(128)} %constant.166.clone.1), dimensions={} | broadcast | bytes 8388612 | tf_op jit(solution)/shard_map/broadcast.14
  227.1 50.0 %while.61 = (s32[]{:T(128)}, f32[16,256,64]{2,1,0:T(8,128)S(1)}, f32[8,16,256,64]{3,2,1,0:T(8,128)}, f32[8,16]{1,0:T(8,128)S(1)}, f32[8,16,1,1]{1,3,2,0:T(1,128)...) while((s32[]{:T(128)}, f32[16,256,64]{2,1,0:T(8,128)S(1)}, ...), condition=%wide.region_5.6_spmd, body=%wide.region_4.5_spmd.sunk | while | flops 524290 | bytes 14681937 | solution.py:57
  277.2 12.8 %copy.134 = f32[8,16,256,64]{2,3,1,0:T(8,128)} copy(f32[8,16,256,64]{3,2,1,0:T(8,128)} %get-tuple-element.804) | data formatting | bytes 16777216 | tf_op jit(solution)/shard_map/jvp()/while | solution.py:57
  290.0 6.6 fusion.123
  296.6 9.6 %fusion.25 = f32[8,128,16,64]{1,3,2,0:T(8,128)S(1)} fusion(f32[8,128,16,64]{1,3,2,0:T(8,128)S(1)} %bitcast.260, f32[8,128,16,64]{1,0,3,2:T(8,128)S(1)} %bitcast.240, f32[16]{0:T(128)S(1)} %copy-done.37, f32[8,128,16]{1,2,0:T(8,128)S(1)} %copy.135, bf16[8,128,16,64]{1,0,3,2:T(8,128)(2,1)S(1)} %bitcast.264, f32[16,8,128]{2,0,1:T(8,128)S(1)} %bitcast.280, ...), kind=kOutput, calls=%fused_computation.54 | convolution fusion | flops 1623195648 | bytes 15417408 | tf_op jit(solution)/shard_map/jvp(kcij,cjkp->cikp)/dot_general | solution.py:46
  306.3 3.3 copy.137
  309.6 6.2 fusion.22
  324.1 19.9 %fusion.78 = f32[8,128,256]{2,1,0:T(8,128)S(1)} fusion(f32[8,16,256,64]{3,2,1,0:T(8,128)} %get-tuple-element.804, f32[8,128,16,64]{1,0,3,2:T(8,128)S(1)} %bitcast.241, f32[8,128,16]{1,2,0:T(8,128)S(1)} %copy.135), kind=kOutput, calls=%fused_computation.99 | convolution fusion | flops 3222274048 | bytes 13697024 | tf_op jit(solution)/shard_map/transpose(jvp(cin,cknp->cikp))/dot_general | solution.py:58
  344.1 14.1 %fusion.16 = (f32[16,8,128]{2,0,1:T(8,128)S(1)}, f32[16,8,128]{2,0,1:T(8,128)S(1)}, f32[16,8,128]{2,0,1:T(8,128)}, f32[8,128,128]{2,1,0:T(8,128)S(1)}) fusion(f32[16,8,128]{2,0,1:T(8,128)S(1)} %bitcast.281, f32[16,8,128]{2,0,1:T(8,128)S(1)} %copy.121, f32[8,128,128]{2,1,0:T(8,128)S(1)} %copy-done.24, pred[128,128]{1,0:T(8,128)(4,1)S(1)} %copy-done.31, ...), kind=kOutput, calls=%fused_computation.42 | convolution fusion | flops 1637695488 | bytes 7684096 | tf_op jit(solution)/shard_map/transpose(jvp(kcij,cjkp->cikp))/dot_general | solution.py:46
  362.3 9.0 %fusion.59 = f32[8,16,256,64]{2,3,1,0:T(8,128)} fusion(bf16[8,128,256,1]{2,1,3,0:T(8,128)(2,1)S(1)} %bitcast.254, f32[8,128,16,64]{1,0,3,2:T(8,128)} %bitcast.243, f32[8,128,16]{1,2,0:T(8,128)S(1)} %copy.135), kind=kOutput, calls=%fused_computation.89 | convolution fusion | flops 3222274048 | bytes 13172736 | tf_op jit(solution)/shard_map/transpose(jvp(cin,cknp->cikp))/dot_general | solution.py:58
  371.4 64.2 %all-gather.14.cloned.1.call-done = bf16[128,256,64]{1,2,0:T(8,128)(2,1)} async-done(((bf16[16,256,64]{1,2,0:T(8,128)(2,1)}), bf16[128,256,64]{1,2,0:T(8,128)(2,1)}) %all-gather.14.cloned.1.call-update) | async-done | bytes 4194320 | tf_op jit(solution)/shard_map/all_gather | solution.py:20
  435.8 25.1 %while.62 = (s32[]{:T(128)}, f32[16,256,64]{2,1,0:T(8,128)S(1)}, s32[]{:T(128)}, bf16[8,16]{1,0:T(8,128)(2,1)S(1)}, bf16[8,16,256,64]{2,3,1,0:T(8,128)(2,1)}, /*index=5*/s32[]{:T(128)}, s32[]{:T(128)}, s32[]{:T(128)}, s32[]{:T(128)}) while((s32[]{:T(128)}, f32[16,256,64]{2,1,0:T(8,128)S(1)}, s32[]{:T(128)}, bf16[8,16]{1,0:T(8,128)(2,1)S(1)}, ...), condition=%wide.region_7.8_spmd, body=%wide.region_6.7_spmd.sunk | while | flops 786454 | bytes 4718907 | solution.py:35
  460.9 8.2 %broadcast.36 = f32[8,16,256,64]{3,2,1,0:T(8,128)} broadcast(f32[]{:T(128)} %constant.166.clone.1), dimensions={} | broadcast | bytes 8388612 | tf_op jit(solution)/shard_map/broadcast.14
  469.1 65.7 %while.63 = (s32[]{:T(128)}, f32[16,256,64]{2,1,0:T(8,128)S(1)}, f32[8,16]{1,0:T(8,128)S(1)}, f32[8,16,256,64]{3,2,1,0:T(8,128)}, f32[8,16,256,64]{2,3,1,0:T(8,1...) while((s32[]{:T(128)}, f32[16,256,64]{2,1,0:T(8,128)S(1)}, ...), condition=%wide.region_10.11_spmd, body=%wide.region_8.10_spmd.sunk | while | flops 1048579 | bytes 15729389 | solution.py:57
  534.9 22.4 %fusion.81 = f32[8,128,256]{2,1,0:T(8,128)S(1)} fusion(f32[8,16,256,64]{3,2,1,0:T(8,128)} %get-tuple-element.342, f32[8,128,16,64]{1,0,3,2:T(8,128)} %bitcast.238, f32[8,128,16]{1,2,0:T(8,128)S(1)} %copy.131), kind=kOutput, calls=%fused_computation.100 | convolution fusion | flops 3222274048 | bytes 13697024 | tf_op jit(solution)/shard_map/transpose(jvp(cjn,cjkp->cknp))/dot_general | solution.py:50
  561.3 4.1 copy.164
  568.5 4.8 multiply_reduce_fusion.2
  573.5 23.4 %multiply_reduce_fusion.3 = (f32[8,128,16]{1,2,0:T(8,128)S(1)}, f32[8,128,16,64]{1,3,2,0:T(8,128)}) fusion(f32[8,128,16,64]{1,0,3,2:T(8,128)} %bitcast.239, bf16[8,128,256,1]{2,1,3,0:T(8,128)(2,1)S(1)} %bitcast.259, f32[8,16,256,64]{3,2,1,0:T(8,128)} %get-tuple-element.342), kind=kOutput, calls=%fused_computation.57 | convolution fusion | flops 3223306240 | bytes 17367040 | tf_op jit(solution)/shard_map/transpose(jvp(cjn,cjkp->cknp))/dot_general | solution.py:50
  597.4 13.5 %fusion.24 = bf16[8,128,16,64]{1,3,2,0:T(8,128)(2,1)S(1)} fusion(f32[8,128,16,64]{1,3,2,0:T(8,128)} %get-tuple-element.552, f32[8,128,16,64]{1,0,3,2:T(8,128)} %bitcast.245, f32[16]{0:T(128)S(1)} %copy-done.38, f32[8,128,16]{1,2,0:T(8,128)S(1)} %copy.131, f32[16,8,128]{2,0,1:T(8,128)S(1)} %bitcast.282, f32[16,8,128]{2,0,1:T(8,128)S(1)} %copy.121, ...), kind=kOutput, calls=%fused_computation.52 | convolution fusion | flops 1624244224 | bytes 15417408 | tf_op jit(solution)/shard_map/transpose(jvp(kcij,cjkp->cikp))/dot_general | solution.py:46
  610.9 4.3 copy.174
  615.1 6.6 reshape.209
  621.8 19.8 %reduce_window_sum.39 = f32[16,8,128]{2,1,0:T(8,128)S(1)} reduce-window(f32[16,8,128]{2,1,0:T(8,128)S(1)} %fusion.108, f32[]{:T(128)} %constant.166.clone.1), window={size=1x1x128 pad=0_0x0_0x0_127}, to_apply=%region_17.18 | reduce-window | flops 2080768 | bytes 131076 | tf_op jit(solution)/shard_map/transpose(jvp(jit(cumsum)))/reduce_window_sum | solution.py:39
  642.6 22.6 %all-reduce.2 = (f32[16]{0:T(128)}, f32[16]{0:T(128)}, f32[16]{0:T(128)}) all-reduce(f32[16]{0:T(128)S(1)} %negate_multiply_fusion, f32[16]{0:T(128)S(1)} %get-tuple-element.532, f32[16]{0:T(128)S(1)} %reduce_sum.143), channel_id=1, replica_groups=mesh['seq'=8,'head'=16] {'seq'}, use_global_device_ids=true, to_apply=%region_22.23 | all-reduce | flops 48 | bytes 384 | tf_op jit(solution)/shard_map/psum | solution.py:138
  (312 shorter events, 186.4 us)
Async XLA Ops:
  7.2 11.8 %copy-start.33 = (f32[16]{0:T(128)S(1)}, f32[16]{0:T(128)}, u32[]{:S(2)}) copy-start(f32[16]{0:T(128)} %param.23) | copy-start | bytes 196
  7.2 11.8 %copy-start.25 = (bf16[16,1024]{1,0:T(8,128)(2,1)S(1)}, bf16[16,1024]{1,0:T(8,128)(2,1)}, u32[]{:S(2)}) copy-start(bf16[16,1024]{1,0:T(8,128)(2,1)} %param.19) | copy-start | bytes 98308
  7.2 60.5 %all-gather.10.cloned.1.call-start = ((), (), s32[]{:S(2)}) async-start(), calls=%async_computation.3 | async-start | bytes 4456448 | tf_op jit(solution)/shard_map/all_gather | solution.py:100
  7.9 117.1 %all-gather.8.cloned.1.call-start = ((), (), s32[]{:S(2)}) async-start(), calls=%async_computation.2 | async-start | bytes 4456448 | tf_op jit(solution)/shard_map/all_gather | solution.py:101
  8.7 206.0 %all-gather.12.cloned.1.call-start = ((), (), s32[]{:S(2)}) async-start(), calls=%async_computation.6 | async-start | bytes 4718592 | tf_op jit(solution)/shard_map/all_gather | solution.py:20
  14.8 57.1 %copy-start.17 = (f32[16,8,128]{2,1,0:T(8,128)}, f32[16,8,128]{2,1,0:T(8,128)S(1)}, u32[]{:S(2)}) copy-start(f32[16,8,128]{2,1,0:T(8,128)S(1)} %reduce_window_sum.36) | copy-start | bytes 196612
  18.8 82.3 %copy-start.5 = (bf16[1024,1024]{0,1:T(8,128)(2,1)}, bf16[1024,1024]{0,1:T(8,128)(2,1)S(1)}, u32[]{:S(2)}) copy-start(bf16[1024,1024]{0,1:T(8,128)(2,1)S(1)} %copy.124) | copy-start | bytes 6291460
  18.8 53.3 %copy-start.40 = (u32[128]{0:T(128)S(1)}, u32[128]{0:T(128)}, u32[]{:S(2)}) copy-start(u32[128]{0:T(128)} %constant.179) | copy-start | bytes 1540
  68.8 59.2 %copy-start.10 = (bf16[1024,256]{1,0:T(8,128)(2,1)}, bf16[1024,256]{1,0:T(8,128)(2,1)S(1)}, u32[]{:S(2)}) copy-start(bf16[1024,256]{1,0:T(8,128)(2,1)S(1)} %constant_dynamic-slice_fusion.7) | copy-start | bytes 1572868
  71.9 363.8 %all-gather.14.cloned.1.call-start = ((), (), s32[]{:S(2)}) async-start(), calls=%async_computation.7 | async-start | bytes 4718592 | tf_op jit(solution)/shard_map/all_gather | solution.py:20
  104.5 192.0 %copy-start.30 = (pred[128,128]{1,0:T(8,128)(4,1)}, pred[128,128]{1,0:T(8,128)(4,1)S(1)}, u32[]{:S(2)}) copy-start(pred[128,128]{1,0:T(8,128)(4,1)S(1)} %iota_compare_fusion) | copy-start | bytes 49156
  277.2 12.8 %copy-start.8 = (bf16[1024,256]{1,0:T(8,128)(2,1)S(1)}, bf16[1024,256]{1,0:T(8,128)(2,1)}, u32[]{:S(2)}) copy-start(bf16[1024,256]{1,0:T(8,128)(2,1)} %copy-done.7) | copy-start | bytes 1572868
  290.0 6.7 copy-start.24
  290.0 6.7 copy-start.37
  296.6 9.7 %copy-start.13 = (f32[8,128,1024]{1,2,0}, f32[8,128,1024]{1,2,0:S(1)}, u32[]{:S(2)}) copy-start(f32[8,128,1024]{1,2,0:S(1)} %fusion.123) | copy-start | bytes 12582916
  320.8 344.4 %reduce-scatter.5.cloned.1.call-start = ((), (), s32[]{:S(2)}) async-start(), calls=%async_computation.5 | async-start | bytes 4456448 | tf_op jit(solution)/shard_map/reduce_scatter | solution.py:146
  324.0 20.0 %copy-start.3 = (f32[128,8,8,128]{3,2,1,0:T(8,128)}, f32[128,8,8,128]{3,2,1,0:T(8,128)S(1)}, u32[]{:S(2)}) copy-start(f32[128,8,8,128]{3,2,1,0:T(8,128)S(1)} %copy.189) | copy-start | bytes 12582916
  324.1 20.0 %copy-start.31 = (pred[128,128]{1,0:T(8,128)(4,1)S(1)}, pred[128,128]{1,0:T(8,128)(4,1)}, u32[]{:S(2)}) copy-start(pred[128,128]{1,0:T(8,128)(4,1)} %copy-done.30) | copy-start | bytes 49156
  344.0 14.1 %copy-start.11 = (bf16[1024,256]{1,0:T(8,128)(2,1)S(1)}, bf16[1024,256]{1,0:T(8,128)(2,1)}, u32[]{:S(2)}) copy-start(bf16[1024,256]{1,0:T(8,128)(2,1)} %copy-done.10) | copy-start | bytes 1572868
  371.4 293.8 %reduce-scatter.3.cloned.1.call-start = ((), (), s32[]{:S(2)}) async-start(), calls=%async_computation.4 | async-start | bytes 4456448 | tf_op jit(solution)/shard_map/reduce_scatter | solution.py:140
  534.8 22.4 %copy-start.9 = (bf16[1024,256]{1,0:T(8,128)(2,1)S(1)}, bf16[1024,256]{1,0:T(8,128)(2,1)}, u32[]{:S(2)}) copy-start(bf16[1024,256]{1,0:T(8,128)(2,1)} %copy-done.7) | copy-start | bytes 1572868
  534.9 22.4 %copy-start.20 = (f32[8,128,128]{2,1,0:T(8,128)S(1)}, f32[8,128,128]{2,1,0:T(8,128)}, u32[]{:S(2)}) copy-start(f32[8,128,128]{2,1,0:T(8,128)} %copy-done.19) | copy-start | bytes 1572868
  573.5 23.5 %copy-start.23 = (f32[2,8,8,128]{3,2,1,0:T(8,128)S(1)}, f32[2,8,8,128]{3,2,1,0:T(8,128)}, u32[]{:S(2)}) copy-start(f32[2,8,8,128]{3,2,1,0:T(8,128)} %copy-done.22) | copy-start | bytes 196612
  573.5 23.5 %copy-start.18 = (f32[16,8,128]{2,1,0:T(8,128)S(1)}, f32[16,8,128]{2,1,0:T(8,128)}, u32[]{:S(2)}) copy-start(f32[16,8,128]{2,1,0:T(8,128)} %copy-done.17) | copy-start | bytes 196612
  573.5 23.5 %copy-start.28 = (f32[16,8,1]{1,0,2:T(8,128)S(1)}, f32[16,8,1]{1,0,2:T(8,128)}, u32[]{:S(2)}) copy-start(f32[16,8,1]{1,0,2:T(8,128)} %copy-done.27) | copy-start | bytes 1540
  573.5 23.5 %copy-start.29 = (f32[16,8,128]{2,0,1:T(8,128)S(1)}, f32[16,8,128]{2,0,1:T(8,128)}, u32[]{:S(2)}) copy-start(f32[16,8,128]{2,0,1:T(8,128)} %get-tuple-element.473) | copy-start | bytes 196612
  573.5 23.9 %copy-start.32 = (pred[128,128]{1,0:T(8,128)(4,1)S(1)}, pred[128,128]{1,0:T(8,128)(4,1)}, u32[]{:S(2)}) copy-start(pred[128,128]{1,0:T(8,128)(4,1)} %copy-done.30) | copy-start | bytes 49156
  573.5 23.9 %copy-start.38 = (f32[16]{0:T(128)S(1)}, f32[16]{0:T(128)}, u32[]{:S(2)}) copy-start(f32[16]{0:T(128)} %param.24) | copy-start | bytes 196
  615.1 26.5 %copy-start.26 = (bf16[16,1024]{1,0:T(8,128)(2,1)S(1)}, bf16[16,1024]{1,0:T(8,128)(2,1)}, u32[]{:S(2)}) copy-start(bf16[16,1024]{1,0:T(8,128)(2,1)} %param.19) | copy-start | bytes 98308
  615.1 26.5 %copy-start.34 = (f32[16]{0:T(128)S(1)}, f32[16]{0:T(128)}, u32[]{:S(2)}) copy-start(f32[16]{0:T(128)} %param.23) | copy-start | bytes 196
  615.1 26.5 %copy-start.36 = (f32[16]{0:T(128)S(1)}, f32[16]{0:T(128)}, u32[]{:S(2)}) copy-start(f32[16]{0:T(128)} %copy-done.35) | copy-start | bytes 196
  615.1 27.4 %copy-start.39 = (f32[16]{0:T(128)S(1)}, f32[16]{0:T(128)}, u32[]{:S(2)}) copy-start(f32[16]{0:T(128)} %param.22) | copy-start | bytes 196
  (29 other events, 78.8 us)
Sparse Core Ops, SparseCore 0:
  10.5 57.2 all-gather.9
  70.2 54.7 all-gather.7
  126.6 88.0 all-gather.11
  320.9 114.6 all-gather.13
  440.1 83.3 reduce-scatter.4
  561.5 83.3 reduce-scatter.2
where the time goes:
time: 684 us; the launch traced here: 672 us
  waiting for transfers between devices  212 us (31%)
  local copies, waits for them, and re-layouts  199 us (29%)
  matrix products  136 us (20%)
  other arithmetic  68.1 us (10%)
  blocking collectives  40.1 us (6%)
  between operations  15.7 us (2%)
    all_gather x2, waiting for transfers between devices, prefix(): lax.all_gather(a.astype(kind), axis)  142 us
    dot_general x3, matrix products, stretch_scan(): states = jnp.einsum('cjn,cjkp->cknp', b_rows, scaled, precision=highest)  54.9 us
    dynamic_slice x32, local copies, waits for them, and re-layouts, stretch_scan(): final_state, starts = lax.scan(advance, start_state, (totals, states))  52.7 us
    all_gather x1, waiting for transfers between devices, per_device(): lax.all_gather(b_proj, 'head', axis=0, tiled=True)  48.6 us
    unnamed x94, local copies, waits for them, and re-layouts  41.1 us
    dot_general x3, matrix products, stretch_scan(): y_diag = jnp.einsum('kcij,cjkp->cikp', mixing, values, precision=highest)  37.2 us
    dot_general x2, matrix products, stretch_scan(): y_off = jnp.einsum('cin,cknp->cikp', c_rows, starts, precision=highest)  29 us
    another operation x2, other arithmetic, stretch_scan(): cum_decay = jnp.cumsum(decays, axis=2)  24.3 us
  transfers between devices with their start and end apart: 6, of which 4 were waited for; matrix products, arithmetic and copies ran while one was open for 43% of the time, Pallas kernels for 0%

commit v1 on v0

v1 whole, which is shorter than its diff:
```python
import jax
import jax.numpy as jnp
from jax import lax
from jax.experimental import pallas as pl
from jax.experimental.pallas import tpu as pltpu
from jax.sharding import PartitionSpec as P

HEAD_DIM = 64
STATE = 256
GROUPS = 8
L = 128
NC = 8
H = 16
W = H * HEAD_DIM
ROWS = 64
F32, BF = jnp.float32, jnp.bfloat16
MESH = pl.DeviceIdType.MESH
HIGHEST = lax.Precision.HIGHEST
LOG2E = 1.4426950408889634


def dot(a, b, ca, cb, precision=None):
    return lax.dot_general(
        a, b, (((ca,), (cb,)), ((), ())), preferred_element_type=F32, precision=precision
    )


def nn(a, b):
    return dot(a, b, 1, 0)


def nt(a, b):
    return dot(a, b, 1, 1)


def tn(a, b):
    return dot(a, b, 0, 0)


def remote(src, dst, send_sem, recv_sem, device):
    return pltpu.make_async_remote_copy(
        src_ref=src,
        dst_ref=dst,
        send_sem=send_sem,
        recv_sem=recv_sem,
        device_id=device,
        device_id_type=MESH,
    )


def rows_of(index, count):
    return pl.ds(pl.multiple_of(index * count, count), count)


def kernel(
    x_hbm, z_hbm, g_hbm, dt_ref, b_hbm, c_hbm, alog_ref, bias_ref, skip_ref,
    gated_hbm, gx_hbm, gz_hbm, gdt_ref, gb_hbm, gc_hbm, galog_ref, gbias_ref, gskip_ref,
    x_v, z_v, g_v, xp, dy, xw, dyw, dtw, ecw, ww, e_s, dtv, ecv, wv, cumv, cumt,
    elw, prew, postw, skw, bc_v, s_loc, ds_loc, s_acc, yd, dxd, stage, sib, fin, gbc,
    sendf, sendg, recvf, recvg, outf, outg, s_in, ds_in, skipacc, fw, qs, ps, par,
    in_sem, out_sem, loc_sem, a_send, a_recv, f_send, f_recv, xf_send, xf_recv, xg_send, xg_recv,
    rf_send, rf_recv, rg_send, rg_recv, sib_send, sib_recv, fin_send, fin_recv, par_send, par_recv,
    gout_sem,
):
    seq = lax.axis_index("seq")
    hd = lax.axis_index("head")
    core = lax.rem(hd, 2)
    chip = lax.div(hd, 2)
    sibling = (seq, 2 * chip + 1 - core)

    def chip_at(k):
        return lax.rem(chip + k, NC)

    def chip_dev(k):
        return (seq, 2 * chip_at(k) + core)

    def slab_at(k):
        return lax.rem(seq + k, NC)

    def slab_dev(k):
        return (slab_at(k), hd)

    def load(a, c):
        src, dst = ((x_hbm, x_v), (z_hbm, z_v), (g_hbm, g_v))[a]
        return pltpu.make_async_copy(
            src.at[rows_of(c, L)], dst.at[rows_of(c, L)], in_sem.at[a, c]
        )

    def own_bc(t):
        src = (b_hbm, c_hbm)[t]
        return pltpu.make_async_copy(
            src.at[:, rows_of(chip, STATE)], bc_v.at[t, rows_of(hd, ROWS)], loc_sem.at[t]
        )

    for c in range(NC):
        for a in range(3):
            load(a, c).start()
    for t in range(2):
        own_bc(t).start()

    barrier = pltpu.get_barrier_semaphore()
    for k in range(1, NC):
        pl.semaphore_signal(barrier, inc=1, device_id=chip_dev(k), device_id_type=MESH)
        pl.semaphore_signal(barrier, inc=1, device_id=slab_dev(k), device_id_type=MESH)
    pl.semaphore_signal(barrier, inc=1, device_id=sibling, device_id_type=MESH)
    pl.semaphore_wait(barrier, 2 * NC - 1)

    def spread(t, k):
        src = (b_hbm, c_hbm)[t]
        device = sibling if k == 0 else chip_dev(k)
        group = chip if k == 0 else chip_at(k)
        return remote(
            src.at[:, rows_of(group, STATE)],
            bc_v.at[t, rows_of(hd, ROWS)],
            a_send.at[t, k],
            a_recv.at[t, k],
            device,
        )

    def arrived(t, k):
        place = 2 * chip + 1 - core if k == 0 else 2 * lax.rem(chip + NC - k, NC) + core
        return remote(
            b_hbm.at[:, rows_of(chip, STATE)],
            bc_v.at[t, rows_of(place, ROWS)],
            a_send.at[t, k],
            a_recv.at[t, k],
            sibling,
        )

    def forward(k, mine):
        place = 2 * lax.rem(chip + NC - k, NC) + (core if mine else 1 - core)
        block = bc_v.at[:, rows_of(place, ROWS)]
        return remote(block, block, f_send.at[k], f_recv.at[k], sibling)

    for k in list(range(1, NC)) + [0]:
        for t in range(2):
            spread(t, k).start()

    row16 = lax.broadcasted_iota(jnp.int32, (H, L), 0)

    def per_head(ref):
        column = jnp.zeros((H, L), F32)
        for h in range(H):
            column = jnp.where(row16 == h, ref[h], column)
        return jnp.concatenate([column] * NC, axis=0)

    rate = -jnp.exp(per_head(alog_ref))
    raw = dt_ref[...].astype(F32)
    pre = jnp.concatenate([raw[:, L * c : L * c + L] for c in range(NC)], axis=0) + per_head(bias_ref)
    step = jnp.maximum(pre, 0.0) + jnp.log1p(jnp.exp(-jnp.abs(pre)))
    decay = rate * step
    iota0 = lax.broadcasted_iota(jnp.int32, (L, L), 0)
    iota1 = lax.broadcasted_iota(jnp.int32, (L, L), 1)
    upper = (iota0 <= iota1).astype(F32)
    cum = dot(decay, upper, 1, 0, HIGHEST)
    step_r = step.astype(BF)
    ecum = jnp.exp(cum)
    tail = jnp.exp(cum[:, L - 1 : L] - cum)
    cum2 = cum * LOG2E
    cum_t = jnp.transpose(cum2)
    step_t = jnp.transpose(step_r.astype(F32))
    ecum_t = jnp.transpose(ecum)
    tail_t = jnp.transpose(tail)
    for c in range(NC):
        cumv[c] = cum2[H * c : H * c + H]
        cumt[c] = cum_t[:, H * c : H * c + H]
        dtv[c] = step_t[:, H * c : H * c + H].astype(BF)
        ecv[c] = ecum_t[:, H * c : H * c + H].astype(BF)
        wv[c] = tail_t[:, H * c : H * c + H].astype(BF)
    head_of = lax.shift_right_logical(lax.broadcasted_iota(jnp.int32, (H, W), 1), 6)
    onehot = head_of == lax.broadcasted_iota(jnp.int32, (H, W), 0)
    e_s[...] = onehot.astype(BF)
    spread_f = onehot.astype(F32)
    last8 = jnp.concatenate([ecum_t[L - 1 : L, H * c : H * c + H] for c in range(NC)], axis=0)
    elast = dot(last8, spread_f, 1, 0, HIGHEST)
    skip_row = jnp.zeros((1, W), F32)
    for h in range(H):
        skip_row = jnp.where(head_of[0:1] == h, skip_ref[h], skip_row)
    skw[...] = skip_row
    run = jnp.ones((1, W), F32)
    for c in range(NC):
        elw[c] = elast[c : c + 1]
        prew[c] = run
        run = run * elast[c : c + 1]
    slab_decay = run
    run = jnp.ones((1, W), F32)
    for c in reversed(range(NC)):
        postw[c + 1] = run
        run = run * elast[c : c + 1]
    postw[0] = run
    skipacc[...] = jnp.zeros_like(skipacc)

    def prepare(c):
        for a in range(3):
            load(a, c).wait()
        r = rows_of(c, L)
        dt_c, ec_c, w_c = dtv[c], ecv[c], wv[c]
        for p in range(W // 256):
            col = slice(256 * p, 256 * p + 256)
            e_c = e_s[:, col]
            dt_w, ec_w, w_w = nn(dt_c, e_c), nn(ec_c, e_c), nn(w_c, e_c)
            dtw[r, col] = dt_w.astype(BF)
            ecw[r, col] = ec_w.astype(BF)
            ww[r, col] = w_w.astype(BF)
            x_r = (x_v[r, col].astype(F32) * dt_w).astype(BF)
            xp[r, col] = x_r
            xw[r, col] = (x_r.astype(F32) * w_w).astype(BF)
            z = z_v[r, col].astype(F32)
            dy_r = (g_v[r, col].astype(F32) * (z / (1.0 + jnp.exp(-z)))).astype(BF)
            dy[r, col] = dy_r
            dyw[r, col] = (dy_r.astype(F32) * ec_w).astype(BF)

    def prepare_step(c, carry):
        prepare(c)
        return carry

    lax.fori_loop(0, NC, prepare_step, 0)
    for k in range(1, NC):
        for t in range(2):
            arrived(t, k).wait_recv()
        forward(k, True).start()
    for t in range(2):
        own_bc(t).wait()
        arrived(t, 0).wait_recv()
    for k in range(1, NC):
        forward(k, False).wait_recv()

    def scan_state(first, keep, t, source, order):
        s_acc[...] = jnp.zeros_like(s_acc)

        def one(i, carry):
            c = order(i)
            r = rows_of(c, L)
            rows_t = jnp.transpose(bc_v[t, r, :])
            for p in range(W // 256):
                col = slice(256 * p, 256 * p + 256)
                now = s_acc[:, col]
                keep[c + first, :, col] = now.astype(BF)
                s_acc[:, col] = elw[c][:, col] * now + nn(rows_t, source[r, col])
            return carry

        lax.fori_loop(0, NC, one, 0)

    def to_joiner(src, dst, send_sem, recv_sem, k):
        return remote(src.at[slab_at(k)], dst.at[seq], send_sem.at[k], recv_sem.at[k], slab_dev(k))

    def from_slab(src, dst, send_sem, recv_sem, k):
        place = lax.rem(seq + NC - k, NC)
        return remote(src.at[place], dst.at[place], send_sem.at[k], recv_sem.at[k], slab_dev(k))

    scan_state(0, s_loc, 0, xw, lambda i: i)
    high = slab_decay.astype(BF).astype(F32)
    decay_rows = jnp.concatenate(
        [high, slab_decay - high, jnp.zeros((14, W), F32)], axis=0
    ).astype(BF)
    for d in range(NC):
        col = slice(128 * d, 128 * d + 128)
        sendf[d, 0:STATE] = s_acc[:, col].astype(BF)
        sendf[d, STATE : STATE + 16] = decay_rows[:, col]
    for k in range(1, NC):
        to_joiner(sendf, recvf, xf_send, xf_recv, k).start()
    recvf[seq] = sendf[seq]

    scan_state(1, ds_loc, 1, dyw, lambda i: NC - 1 - i)
    for p in range(W // 256):
        col = slice(256 * p, 256 * p + 256)
        ds_loc[0, :, col] = s_acc[:, col].astype(BF)
    for d in range(NC):
        sendg[d] = s_acc[:, 128 * d : 128 * d + 128].astype(BF)
    for k in range(1, NC):
        to_joiner(sendg, recvg, xg_send, xg_recv, k).start()
    recvg[seq] = sendg[seq]

    low = iota0 >= iota1
    lane = lax.broadcasted_iota(jnp.int32, (1, L), 1)
    left = (lane < HEAD_DIM).astype(F32)
    left_b = left.astype(BF)
    right_b = (1.0 - left).astype(BF)

    def intra(c, carry):
        r = rows_of(c, L)
        b_c, c_c = bc_v[0, r, :], bc_v[1, r, :]
        scores = jnp.where(low, nt(c_c, b_c), 0.0)
        d_scores = jnp.zeros((L, L), F32)
        cum_r, cum_c = cumv[c], cumt[c]
        for p in range(H // 2):
            col = slice(L * p, L * p + L)
            x_p, dy_p = xp[r, col], dy[r, col]
            x_two = jnp.concatenate([x_p * left_b, x_p * right_b], axis=0)
            d_mix = nt(dy_p, x_two)
            parts = []
            for j in range(2):
                h = 2 * p + j
                seg = cum_c[:, h : h + 1] - cum_r[h : h + 1, :]
                mask = jnp.exp2(jnp.minimum(seg, 0.0))
                parts.append((scores * mask).astype(BF))
                d_scores = d_scores + d_mix[:, L * j : L * j + L] * mask
            mix = jnp.concatenate(parts, axis=1)
            yd[r, col] = nn(mix, x_two)
            both = tn(mix, dy_p)
            dxd[r, col] = jnp.where(left > 0.0, both[:L], both[L:])
        d_scores = jnp.where(low, d_scores, 0.0).astype(BF)
        stage[c, 0] = tn(d_scores, c_c)
        stage[c, 1] = nn(d_scores, b_c)
        return carry

    lax.fori_loop(0, NC // 2, intra, 0)

    for k in range(1, NC):
        from_slab(sendf, recvf, xf_send, xf_recv, k).wait_recv()
    run = jnp.zeros((STATE, L), F32)
    for i in range(NC):
        outf[i] = run.astype(BF)
        factor = recvf[i, STATE : STATE + 16].astype(F32)
        run = (factor[0:1] + factor[1:2]) * run + recvf[i, 0:STATE].astype(F32)

    def back(src, dst, send_sem, recv_sem, k):
        return remote(
            src.at[slab_at(k)], dst.at[seq], send_sem.at[k], recv_sem.at[k], slab_dev(k)
        )

    for k in range(1, NC):
        back(outf, s_in, rf_send, rf_recv, k).start()
    s_in[seq] = outf[seq]
    for k in range(1, NC):
        from_slab(sendg, recvg, xg_send, xg_recv, k).wait_recv()
    run = jnp.zeros((STATE, L), F32)
    for i in reversed(range(NC)):
        outg[i] = run.astype(BF)
        factor = recvf[i, STATE : STATE + 16].astype(F32)
        run = (factor[0:1] + factor[1:2]) * run + recvg[i].astype(F32)
    for k in range(1, NC):
        back(outg, ds_in, rg_send, rg_recv, k).start()
    ds_in[seq] = outg[seq]

    lax.fori_loop(NC // 2, NC, intra, 0)

    for k in range(1, NC):
        from_slab(outf, s_in, rf_send, rf_recv, k).wait_recv()
        from_slab(outg, ds_in, rg_send, rg_recv, k).wait_recv()

    def to_sibling(k):
        c = chip_at(k)
        return remote(
            stage.at[c, :, rows_of(1 - core, ROWS)], sib.at[c], sib_send.at[k], sib_recv.at[k], sibling
        )

    def to_owner(k):
        return remote(
            fin.at[chip_at(k)],
            gbc.at[:, :, rows_of(chip, STATE)],
            fin_send.at[k],
            fin_recv.at[k],
            chip_dev(k),
        )

    def from_group(k):
        return remote(
            fin.at[chip_at(k)],
            gbc.at[:, :, rows_of(lax.rem(chip + NC - k, NC), STATE)],
            fin_send.at[k],
            fin_recv.at[k],
            sibling,
        )

    def store(a, c):
        src, dst = ((x_v, gx_hbm), (z_v, gated_hbm), (g_v, gz_hbm))[a]
        return pltpu.make_async_copy(
            src.at[rows_of(c, L)], dst.at[rows_of(c, L)], out_sem.at[a, c]
        )

    def settle(k):
        c = chip_at(k)
        to_sibling(k).wait_recv()
        total = (stage[c, :, rows_of(core, ROWS)] + sib[c]).astype(BF)

        @pl.when(k == 0)
        def _():
            gbc[:, :, rows_of(chip, STATE)] = total

        @pl.when(k > 0)
        def _():
            fin[c] = total
            to_owner(k).start()

    def finish(k, carry):
        c = chip_at(k)
        r = rows_of(c, L)
        b_c, c_c = bc_v[0, r, :], bc_v[1, r, :]
        d_b, d_c = stage[c, 0], stage[c, 1]
        q = jnp.zeros((H, L), F32)
        px = jnp.zeros((H, L), F32)
        for p in range(W // 256):
            col = slice(256 * p, 256 * p + 256)
            start = jnp.concatenate([s_in[2 * p], s_in[2 * p + 1]], axis=1).astype(F32)
            end = jnp.concatenate([ds_in[2 * p], ds_in[2 * p + 1]], axis=1).astype(F32)
            s_t = s_loc[c, :, col].astype(F32) + prew[c][:, col] * start
            ds_t = ds_loc[c + 1, :, col].astype(F32) + postw[c + 1][:, col] * end
            ds_p = ds_loc[c, :, col].astype(F32) + postw[c][:, col] * end
            fw[c, :, col] = jnp.sum(s_t * ds_p, axis=0, keepdims=True)
            s_b, ds_b = s_t.astype(BF), ds_t.astype(BF)
            d_c = d_c + nt(dyw[r, col], s_b)
            d_b = d_b + nt(xw[r, col], ds_b)
            y_core = yd[r, col] + ecw[r, col].astype(F32) * nn(c_c, s_b)
            dx = dxd[r, col] + ww[r, col].astype(F32) * nn(b_c, ds_b)
            e_c = e_s[:, col]
            p_x = xp[r, col].astype(F32) * dx
            q_x = dy[r, col].astype(F32) * y_core - p_x
            q_h = q_x.astype(BF)
            q_l = (q_x - q_h.astype(F32)).astype(BF)
            q = q + nt(e_c, q_h) + nt(e_c, q_l)
            px = px + nt(e_c, p_x.astype(BF))
            x, z, g = (v[r, col].astype(F32) for v in (x_v, z_v, g_v))
            skip = skw[:, col]
            sig = 1.0 / (1.0 + jnp.exp(-z))
            silu = z * sig
            y = y_core + skip * x
            dy_f = g * silu
            z_v[r, col] = (y * silu).astype(BF)
            g_v[r, col] = (g * y * (sig + silu * (1.0 - sig))).astype(BF)
            x_v[r, col] = (skip * dy_f + dtw[r, col].astype(F32) * dx).astype(BF)
            skipacc[:, col] += jnp.sum((dy_f * x).reshape(L // 8, 8, 256), axis=0)
        stage[c, 0] = d_b
        stage[c, 1] = d_c
        qs[c] = q
        ps[c] = px
        for a in range(3):
            store(a, c).start()
        to_sibling(k).start()

        @pl.when(k > 0)
        def _():
            settle(k - 1)

        return carry

    lax.fori_loop(0, NC, finish, 0)
    settle(NC - 1)

    q = qs[...].reshape(L, L)
    px = ps[...].reshape(L, L)
    before = dot(q, (iota0 < iota1).astype(F32), 1, 0, HIGHEST)
    pairs = dot(spread_f, fw[...].reshape(NC, W), 1, 1, HIGHEST)
    boundary = jnp.concatenate([pairs[:, c : c + 1] for c in range(NC)], axis=0)
    d_decay = boundary - before
    d_step = px / step_r.astype(F32) + rate * d_decay
    d_raw = d_step / (1.0 + jnp.exp(-pre))
    for c in range(NC):
        gdt_ref[:, L * c : L * c + L] = d_raw[H * c : H * c + H].astype(BF)

    def over_tokens(v):
        column = jnp.sum(v, axis=1, keepdims=True)
        total = column[0:H]
        for c in range(1, NC):
            total = total + column[H * c : H * c + H]
        return total

    skip_sum = jnp.sum(dot(spread_f, skipacc[...], 1, 1, HIGHEST), axis=1, keepdims=True)
    lane16 = lax.broadcasted_iota(jnp.int32, (H, L), 1)
    par[0] = jnp.where(
        lane16 == 0,
        over_tokens(d_decay * decay),
        jnp.where(lane16 == 1, over_tokens(d_raw), skip_sum),
    )

    def share(k):
        return remote(par.at[0], par.at[k], par_send.at[k], par_recv.at[k], slab_dev(k))

    for k in range(1, NC):
        share(k).start()
    for k in range(1, NC):
        from_group(k).wait_recv()
    outs = [
        pltpu.make_async_copy(gbc.at[0], gb_hbm, gout_sem.at[0]),
        pltpu.make_async_copy(gbc.at[1], gc_hbm, gout_sem.at[1]),
    ]
    for o in outs:
        o.start()
    for k in range(1, NC):
        share(k).wait_recv()
    total = par[0]
    for k in range(1, NC):
        total = total + par[k]
    flat = jnp.transpose(jnp.concatenate([total] * NC, axis=0))
    galog_ref[...] = flat[0:1, 0:H]
    gbias_ref[...] = flat[1:2, 0:H]
    gskip_ref[...] = flat[2:3, 0:H]

    for o in outs:
        o.wait()
    for k in range(NC):
        for t in range(2):
            spread(t, k).wait_send()
        to_sibling(k).wait_send()
    for k in range(1, NC):
        forward(k, True).wait_send()
        to_joiner(sendf, recvf, xf_send, xf_recv, k).wait_send()
        to_joiner(sendg, recvg, xg_send, xg_recv, k).wait_send()
        back(outf, s_in, rf_send, rf_recv, k).wait_send()
        back(outg, ds_in, rg_send, rg_recv, k).wait_send()
        to_owner(k).wait_send()
        share(k).wait_send()
    for c in range(NC):
        for a in range(3):
            store(a, c).wait()


def per_device(inner_x, gate_z, dt_raw, b_proj, c_proj, a_log, dt_bias, d_skip, grad_gated):
    tokens = inner_x.shape[0]
    any_space = pl.BlockSpec(memory_space=pl.ANY)
    vmem = pl.BlockSpec(memory_space=pltpu.VMEM)
    smem = pl.BlockSpec(memory_space=pltpu.SMEM)
    sem = pltpu.SemaphoreType.DMA
    big = jax.ShapeDtypeStruct((tokens, W), BF)
    rows = jax.ShapeDtypeStruct((ROWS, GROUPS * STATE), BF)
    head = jax.ShapeDtypeStruct((1, H), F32)
    wide = pltpu.VMEM((tokens, W), BF)
    scratch = [
        wide, wide, wide,
        wide, wide, wide, wide,
        wide, wide, wide,
        pltpu.VMEM((H, W), BF),
        pltpu.VMEM((NC, L, H), BF),
        pltpu.VMEM((NC, L, H), BF),
        pltpu.VMEM((NC, L, H), BF),
        pltpu.VMEM((NC, H, L), F32),
        pltpu.VMEM((NC, L, H), F32),
        pltpu.VMEM((NC, 1, W), F32),
        pltpu.VMEM((NC, 1, W), F32),
        pltpu.VMEM((NC + 1, 1, W), F32),
        pltpu.VMEM((1, W), F32),
        pltpu.VMEM((2, tokens, STATE), BF),
        pltpu.VMEM((NC, STATE, W), BF),
        pltpu.VMEM((NC + 1, STATE, W), BF),
        pltpu.VMEM((STATE, W), F32),
        pltpu.VMEM((tokens, W), F32),
        pltpu.VMEM((tokens, W), F32),
        pltpu.VMEM((NC, 2, L, STATE), F32),
        pltpu.VMEM((NC, 2, ROWS, STATE), F32),
        pltpu.VMEM((NC, 2, ROWS, STATE), BF),
        pltpu.VMEM((2, ROWS, GROUPS * STATE), BF),
        pltpu.VMEM((NC, STATE + 16, L), BF),
        pltpu.VMEM((NC, STATE, L), BF),
        pltpu.VMEM((NC, STATE + 16, L), BF),
        pltpu.VMEM((NC, STATE, L), BF),
        pltpu.VMEM((NC, STATE, L), BF),
        pltpu.VMEM((NC, STATE, L), BF),
        pltpu.VMEM((NC, STATE, L), BF),
        pltpu.VMEM((NC, STATE, L), BF),
        pltpu.VMEM((8, W), F32),
        pltpu.VMEM((NC, 1, W), F32),
        pltpu.VMEM((NC, H, L), F32),
        pltpu.VMEM((NC, H, L), F32),
        pltpu.VMEM((NC, H, L), F32),
        sem((3, NC)), sem((3, NC)), sem((2,)),
        sem((2, NC)), sem((2, NC)), sem((NC,)), sem((NC,)),
        sem((NC,)), sem((NC,)), sem((NC,)), sem((NC,)),
        sem((NC,)), sem((NC,)), sem((NC,)), sem((NC,)),
        sem((NC,)), sem((NC,)), sem((NC,)), sem((NC,)), sem((NC,)), sem((NC,)),
        sem((2,)),
    ]
    outs = pl.pallas_call(
        kernel,
        out_shape=(big, big, big, jax.ShapeDtypeStruct((H, tokens), BF), rows, rows, head, head, head),
        in_specs=[any_space, any_space, any_space, vmem, any_space, any_space, smem, smem, smem],
        out_specs=(any_space, any_space, any_space, vmem, any_space, any_space, vmem, vmem, vmem),
        scratch_shapes=scratch,
        compiler_params=pltpu.CompilerParams(
            collective_id=0, has_side_effects=True, vmem_limit_bytes=60 * 2**20
        ),
    )(inner_x, gate_z, grad_gated, dt_raw, b_proj, c_proj, a_log, dt_bias, d_skip)
    gated, grad_x, grad_z, grad_dt, grad_b, grad_c, g_alog, g_bias, g_skip = outs
    return (
        gated, grad_x, grad_z, grad_dt, grad_b, grad_c,
        g_alog.reshape(H), g_bias.reshape(H), g_skip.reshape(H),
    )


def solution(mesh):
    in_specs = (
        P("seq", "head"),
        P("seq", "head"),
        P("head", "seq"),
        P(("seq", "head"), None),
        P(("seq", "head"), None),
        P("head"),
        P("head"),
        P("head"),
        P("seq", "head"),
    )
    out_specs = (
        P("seq", "head"),
        P("seq", "head"),
        P("seq", "head"),
        P("head", "seq"),
        P(("seq", "head"), None),
        P(("seq", "head"), None),
        P("head"),
        P("head"),
        P("head"),
    )
    return jax.shard_map(
        per_device, mesh=mesh, in_specs=in_specs, out_specs=out_specs, check_vma=False
    )
```

time: 684 us -> 81.1 us (0.12)
  the two profiles are of different devices: /device:TPU:32 before, /device:TPU:1 now
where the time goes in v1:
time: 81.1 us; the launch traced here: 80.1 us
  Pallas kernels  69 us (85%)
  local copies, waits for them, and re-layouts  10.5 us (13%)
    pallas_call x1, Pallas kernels, per_device(): pl.pallas_call(kernel, out_shape=(big, big, big, jax.ShapeDtypeStruct((H,...  69 us
    unnamed x25, local copies, waits for them, and re-layouts  10.5 us

profile of v1, /device:TPU:1, one launch (start us, length us, event | category | flops | bytes accessed | tf_op | source)
XLA Modules:
  0.0 80.1 jit_solution(11831421388287706440)
XLA Ops:
  0.6 69.0 %shard_map.160 = (bf16[1024,1024]{1,0:T(8,128)(2,1)}, bf16[1024,1024]{1,0:T(8,128)(2,1)}, bf16[1024,1024]{1,0:T(8,128)(2,1)}, bf16[16,1024]{1,0:T(8,128)(2,1)}, ...) custom-call(bf16[1024,1024]{1,0:T(8,128)(2,1)} %x_hbm.1, ...), custom_call_target="tpu_custom_call" | custom-call | tf_op jit(solution)/shard_map/pallas_call | solution.py:562
  69.6 0.0 copy-start.1
  69.6 3.2 %copy.27 = bf16[1024,1024]{1,0:T(8,128)(2,1)} copy(bf16[1024,1024]{1,0:T(8,128)(2,1)} %get-tuple-element.36) | data formatting | bytes 4194304
  72.9 0.0 copy-done.1
  72.9 0.0 copy-start
  72.9 1.3 %copy.28 = bf16[1024,1024]{1,0:T(8,128)(2,1)} copy(bf16[1024,1024]{1,0:T(8,128)(2,1)S(1)} %copy-done.1) | data formatting | bytes 4194304
  74.2 1.0 %copy-done = bf16[1024,1024]{1,0:T(8,128)(2,1)S(1)} copy-done((bf16[1024,1024]{1,0:T(8,128)(2,1)S(1)}, bf16[1024,1024]{1,0:T(8,128)(2,1)}, u32[]{:S(2)}) %copy-start) | copy-done | bytes 2097176
  75.2 0.0 copy-start.4
  75.2 0.0 copy-start.3
  75.2 0.0 copy-start.2
  75.2 0.0 copy-start.7
  75.2 0.0 copy-start.6
  75.2 0.0 copy-start.5
  75.3 1.3 %copy.29 = bf16[1024,1024]{1,0:T(8,128)(2,1)} copy(bf16[1024,1024]{1,0:T(8,128)(2,1)S(1)} %copy-done) | data formatting | bytes 4194304
  76.6 0.0 copy-done.4
  76.6 0.6 copy.30
  77.2 0.0 copy-done.3
  77.2 0.7 copy.31
  77.9 0.0 copy-done.2
  77.9 0.7 copy.32
  78.6 0.0 copy-done.7
  78.6 0.5 copy.33
  79.1 0.0 copy-done.6
  79.1 0.5 copy.34
  79.6 0.0 copy-done.5
  79.6 0.5 copy.35
Async XLA Ops:
  69.6 3.2 %copy-start.1 = (bf16[1024,1024]{1,0:T(8,128)(2,1)S(1)}, bf16[1024,1024]{1,0:T(8,128)(2,1)}, u32[]{:S(2)}) copy-start(bf16[1024,1024]{1,0:T(8,128)(2,1)} %get-tuple-element.37) | copy-start | bytes 6291460
  72.9 2.3 %copy-start = (bf16[1024,1024]{1,0:T(8,128)(2,1)S(1)}, bf16[1024,1024]{1,0:T(8,128)(2,1)}, u32[]{:S(2)}) copy-start(bf16[1024,1024]{1,0:T(8,128)(2,1)} %get-tuple-element.38) | copy-start | bytes 6291460
  75.2 1.4 %copy-start.4 = (bf16[16,1024]{1,0:T(8,128)(2,1)S(1)}, bf16[16,1024]{1,0:T(8,128)(2,1)}, u32[]{:S(2)}) copy-start(bf16[16,1024]{1,0:T(8,128)(2,1)} %get-tuple-element.39) | copy-start | bytes 98308
  75.2 2.0 %copy-start.3 = (bf16[64,2048]{1,0:T(8,128)(2,1)S(1)}, bf16[64,2048]{1,0:T(8,128)(2,1)}, u32[]{:S(2)}) copy-start(bf16[64,2048]{1,0:T(8,128)(2,1)} %get-tuple-element.40) | copy-start | bytes 786436
  75.2 2.7 %copy-start.2 = (bf16[64,2048]{1,0:T(8,128)(2,1)S(1)}, bf16[64,2048]{1,0:T(8,128)(2,1)}, u32[]{:S(2)}) copy-start(bf16[64,2048]{1,0:T(8,128)(2,1)} %get-tuple-element.41) | copy-start | bytes 786436
  75.2 3.4 %copy-start.7 = (f32[1,16]{1,0:T(1,128)S(1)}, f32[1,16]{1,0:T(1,128)}, u32[]{:S(2)}) copy-start(f32[1,16]{1,0:T(1,128)} %get-tuple-element.24) | copy-start | bytes 196
  75.2 3.9 %copy-start.6 = (f32[1,16]{1,0:T(1,128)S(1)}, f32[1,16]{1,0:T(1,128)}, u32[]{:S(2)}) copy-start(f32[1,16]{1,0:T(1,128)} %get-tuple-element.25) | copy-start | bytes 196
  75.2 4.4 %copy-start.5 = (f32[1,16]{1,0:T(1,128)S(1)}, f32[1,16]{1,0:T(1,128)}, u32[]{:S(2)}) copy-start(f32[1,16]{1,0:T(1,128)} %get-tuple-element.26) | copy-start | bytes 196

commit v2 on v1

--- a/solution.py
+++ b/solution.py
@@ -16,6 +16,7 @@
 F32, BF = jnp.float32, jnp.bfloat16
 MESH = pl.DeviceIdType.MESH
 HIGHEST = lax.Precision.HIGHEST
+AROUND = (5, 4, 3, 2, 7, 6, 1)
 LOG2E = 1.4426950408889634
 
 
@@ -64,18 +65,24 @@
 ):
     seq = lax.axis_index("seq")
     hd = lax.axis_index("head")
-    core = lax.rem(hd, 2)
-    chip = lax.div(hd, 2)
+    core = hd & 1
+    chip = hd >> 1
     sibling = (seq, 2 * chip + 1 - core)
 
     def chip_at(k):
-        return lax.rem(chip + k, NC)
+        return ((chip + k) & 3) | ((chip ^ k) & 4)
+
+    def chip_back(k):
+        return ((chip - k) & 3) | ((chip ^ k) & 4)
 
     def chip_dev(k):
         return (seq, 2 * chip_at(k) + core)
 
     def slab_at(k):
-        return lax.rem(seq + k, NC)
+        return ((seq + (k & 6)) & 6) | ((seq ^ k) & 1)
+
+    def slab_back(k):
+        return ((seq - (k & 6)) & 6) | ((seq ^ k) & 1)
 
     def slab_dev(k):
         return (slab_at(k), hd)
@@ -118,7 +125,7 @@
         )
 
     def arrived(t, k):
-        place = 2 * chip + 1 - core if k == 0 else 2 * lax.rem(chip + NC - k, NC) + core
+        place = 2 * chip + 1 - core if k == 0 else 2 * chip_back(k) + core
         return remote(
             b_hbm.at[:, rows_of(chip, STATE)],
             bc_v.at[t, rows_of(place, ROWS)],
@@ -127,14 +134,25 @@
             sibling,
         )
 
-    def forward(k, mine):
-        place = 2 * lax.rem(chip + NC - k, NC) + (core if mine else 1 - core)
-        block = bc_v.at[:, rows_of(place, ROWS)]
-        return remote(block, block, f_send.at[k], f_recv.at[k], sibling)
-
-    for k in list(range(1, NC)) + [0]:
-        for t in range(2):
+    def forward(t, k, mine):
+        place = 2 * chip_back(k) + (core if mine else 1 - core)
+        block = bc_v.at[t, rows_of(place, ROWS)]
+        return remote(block, block, f_send.at[t, k], f_recv.at[t, k], sibling)
+
+    for t in range(2):
+        for k in (6, 5, 7, 4, 2, 1, 3, 0):
             spread(t, k).start()
+
+    def pass_on(t):
+        for k in (4, 1, 3, 2, 5, 7, 6):
+            arrived(t, k).wait_recv()
+            forward(t, k, True).start()
+
+    def complete(t):
+        own_bc(t).wait()
+        arrived(t, 0).wait_recv()
+        for k in range(1, NC):
+            forward(t, k, False).wait_recv()
 
     row16 = lax.broadcasted_iota(jnp.int32, (H, L), 0)
 
@@ -153,24 +171,24 @@
     iota1 = lax.broadcasted_iota(jnp.int32, (L, L), 1)
     upper = (iota0 <= iota1).astype(F32)
     cum = dot(decay, upper, 1, 0, HIGHEST)
-    step_r = step.astype(BF)
     ecum = jnp.exp(cum)
     tail = jnp.exp(cum[:, L - 1 : L] - cum)
     cum2 = cum * LOG2E
     cum_t = jnp.transpose(cum2)
-    step_t = jnp.transpose(step_r.astype(F32))
+    step_t = jnp.transpose(step)
     ecum_t = jnp.transpose(ecum)
     tail_t = jnp.transpose(tail)
     for c in range(NC):
         cumv[c] = cum2[H * c : H * c + H]
         cumt[c] = cum_t[:, H * c : H * c + H]
-        dtv[c] = step_t[:, H * c : H * c + H].astype(BF)
-        ecv[c] = ecum_t[:, H * c : H * c + H].astype(BF)
-        wv[c] = tail_t[:, H * c : H * c + H].astype(BF)
+        for keep, value in ((dtv, step_t), (ecv, ecum_t), (wv, tail_t)):
+            column = value[:, H * c : H * c + H]
+            high = column.astype(BF)
+            keep[c] = jnp.concatenate([high.astype(F32), column - high.astype(F32)], axis=1).astype(BF)
     head_of = lax.shift_right_logical(lax.broadcasted_iota(jnp.int32, (H, W), 1), 6)
     onehot = head_of == lax.broadcasted_iota(jnp.int32, (H, W), 0)
-    e_s[...] = onehot.astype(BF)
     spread_f = onehot.astype(F32)
+    e_s[...] = jnp.concatenate([spread_f, spread_f], axis=0).astype(BF)
     last8 = jnp.concatenate([ecum_t[L - 1 : L, H * c : H * c + H] for c in range(NC)], axis=0)
     elast = dot(last8, spread_f, 1, 0, HIGHEST)
     skip_row = jnp.zeros((1, W), F32)
@@ -190,40 +208,39 @@
     postw[0] = run
     skipacc[...] = jnp.zeros_like(skipacc)
 
-    def prepare(c):
-        for a in range(3):
-            load(a, c).wait()
+    def prepare_x(c, carry):
+        load(0, c).wait()
         r = rows_of(c, L)
-        dt_c, ec_c, w_c = dtv[c], ecv[c], wv[c]
+        dt_c, w_c = dtv[c], wv[c]
         for p in range(W // 256):
             col = slice(256 * p, 256 * p + 256)
             e_c = e_s[:, col]
-            dt_w, ec_w, w_w = nn(dt_c, e_c), nn(ec_c, e_c), nn(w_c, e_c)
-            dtw[r, col] = dt_w.astype(BF)
-            ecw[r, col] = ec_w.astype(BF)
-            ww[r, col] = w_w.astype(BF)
-            x_r = (x_v[r, col].astype(F32) * dt_w).astype(BF)
-            xp[r, col] = x_r
-            xw[r, col] = (x_r.astype(F32) * w_w).astype(BF)
+            dt_w, w_w = nn(dt_c, e_c), nn(w_c, e_c)
+            dtw[r, col] = dt_w
+            ww[r, col] = w_w
+            scaled = x_v[r, col].astype(F32) * dt_w
+            xp[r, col] = scaled.astype(BF)
+            xw[r, col] = (scaled * w_w).astype(BF)
+        return carry
+
+    def prepare_g(c, carry):
+        load(1, c).wait()
+        load(2, c).wait()
+        r = rows_of(c, L)
+        ec_c = ecv[c]
+        for p in range(W // 256):
+            col = slice(256 * p, 256 * p + 256)
+            ec_w = nn(ec_c, e_s[:, col])
+            ecw[r, col] = ec_w
             z = z_v[r, col].astype(F32)
-            dy_r = (g_v[r, col].astype(F32) * (z / (1.0 + jnp.exp(-z)))).astype(BF)
-            dy[r, col] = dy_r
-            dyw[r, col] = (dy_r.astype(F32) * ec_w).astype(BF)
-
-    def prepare_step(c, carry):
-        prepare(c)
+            dy_f = g_v[r, col].astype(F32) * (z / (1.0 + jnp.exp(-z)))
+            dy[r, col] = dy_f.astype(BF)
+            dyw[r, col] = (dy_f * ec_w).astype(BF)
         return carry
 
-    lax.fori_loop(0, NC, prepare_step, 0)
-    for k in range(1, NC):
-        for t in range(2):
-            arrived(t, k).wait_recv()
-        forward(k, True).start()
-    for t in range(2):
-        own_bc(t).wait()
-        arrived(t, 0).wait_recv()
-    for k in range(1, NC):
-        forward(k, False).wait_recv()
+    lax.fori_loop(0, NC, prepare_x, 0)
+    pass_on(0)
+    complete(0)
 
     def scan_state(first, keep, t, source, order):
         s_acc[...] = jnp.zeros_like(s_acc)
@@ -245,7 +262,7 @@
         return remote(src.at[slab_at(k)], dst.at[seq], send_sem.at[k], recv_sem.at[k], slab_dev(k))
 
     def from_slab(src, dst, send_sem, recv_sem, k):
-        place = lax.rem(seq + NC - k, NC)
+        place = slab_back(k)
         return remote(src.at[place], dst.at[place], send_sem.at[k], recv_sem.at[k], slab_dev(k))
 
     scan_state(0, s_loc, 0, xw, lambda i: i)
@@ -257,18 +274,27 @@
         col = slice(128 * d, 128 * d + 128)
         sendf[d, 0:STATE] = s_acc[:, col].astype(BF)
         sendf[d, STATE : STATE + 16] = decay_rows[:, col]
-    for k in range(1, NC):
-        to_joiner(sendf, recvf, xf_send, xf_recv, k).start()
+    @pl.when(seq != NC - 1)
+    def _():
+        for k in AROUND:
+            to_joiner(sendf, recvf, xf_send, xf_recv, k).start()
+
     recvf[seq] = sendf[seq]
 
+    pass_on(1)
+    lax.fori_loop(0, NC, prepare_g, 0)
+    complete(1)
     scan_state(1, ds_loc, 1, dyw, lambda i: NC - 1 - i)
     for p in range(W // 256):
         col = slice(256 * p, 256 * p + 256)
         ds_loc[0, :, col] = s_acc[:, col].astype(BF)
     for d in range(NC):
         sendg[d] = s_acc[:, 128 * d : 128 * d + 128].astype(BF)
-    for k in range(1, NC):
-        to_joiner(sendg, recvg, xg_send, xg_recv, k).start()
+    @pl.when(seq != 0)
+    def _():
+        for k in AROUND:
+            to_joiner(sendg, recvg, xg_send, xg_recv, k).start()
+
     recvg[seq] = sendg[seq]
 
     low = iota0 >= iota1
@@ -277,11 +303,18 @@
     left_b = left.astype(BF)
     right_b = (1.0 - left).astype(BF)
 
+    def by_head(v, col):
+        high = v.astype(BF)
+        low_part = (v - high.astype(F32)).astype(BF)
+        e_c = e_s[0:H, col]
+        return nt(e_c, high) + nt(e_c, low_part)
+
     def intra(c, carry):
         r = rows_of(c, L)
         b_c, c_c = bc_v[0, r, :], bc_v[1, r, :]
         scores = jnp.where(low, nt(c_c, b_c), 0.0)
         d_scores = jnp.zeros((L, L), F32)
+        px = jnp.zeros((H, L), F32)
         cum_r, cum_c = cumv[c], cumt[c]
         for p in range(H // 2):
             col = slice(L * p, L * p + L)
@@ -298,68 +331,88 @@
             mix = jnp.concatenate(parts, axis=1)
             yd[r, col] = nn(mix, x_two)
             both = tn(mix, dy_p)
-            dxd[r, col] = jnp.where(left > 0.0, both[:L], both[L:])
+            dx = jnp.where(left > 0.0, both[:L], both[L:])
+            dxd[r, col] = dx
+            px = px + by_head(x_p.astype(F32) * dx, col)
         d_scores = jnp.where(low, d_scores, 0.0).astype(BF)
         stage[c, 0] = tn(d_scores, c_c)
         stage[c, 1] = nn(d_scores, b_c)
+        ps[c] = px
         return carry
 
-    lax.fori_loop(0, NC // 2, intra, 0)
-
-    for k in range(1, NC):
-        from_slab(sendf, recvf, xf_send, xf_recv, k).wait_recv()
+    lax.fori_loop(0, 3, intra, 0)
+
+    def collect(src, dst, send_sem, recv_sem, absent):
+        for k in range(1, NC):
+
+            @pl.when(slab_back(k) != absent)
+            def _():
+                from_slab(src, dst, send_sem, recv_sem, k).wait_recv()
+
+    collect(sendf, recvf, xf_send, xf_recv, NC - 1)
     run = jnp.zeros((STATE, L), F32)
     for i in range(NC):
         outf[i] = run.astype(BF)
-        factor = recvf[i, STATE : STATE + 16].astype(F32)
-        run = (factor[0:1] + factor[1:2]) * run + recvf[i, 0:STATE].astype(F32)
+        if i == 0:
+            run = recvf[0, 0:STATE].astype(F32)
+        elif i < NC - 1:
+            factor = recvf[i, STATE : STATE + 16].astype(F32)
+            run = (factor[0:1] + factor[1:2]) * run + recvf[i, 0:STATE].astype(F32)
 
     def back(src, dst, send_sem, recv_sem, k):
         return remote(
             src.at[slab_at(k)], dst.at[seq], send_sem.at[k], recv_sem.at[k], slab_dev(k)
         )
 
-    for k in range(1, NC):
-        back(outf, s_in, rf_send, rf_recv, k).start()
+    def give_back(src, dst, send_sem, recv_sem, absent):
+        for k in AROUND:
+
+            @pl.when(slab_at(k) != absent)
+            def _():
+                back(src, dst, send_sem, recv_sem, k).start()
+
+    give_back(outf, s_in, rf_send, rf_recv, 0)
     s_in[seq] = outf[seq]
-    for k in range(1, NC):
-        from_slab(sendg, recvg, xg_send, xg_recv, k).wait_recv()
+    lax.fori_loop(3, 6, intra, 0)
+    collect(sendg, recvg, xg_send, xg_recv, 0)
     run = jnp.zeros((STATE, L), F32)
     for i in reversed(range(NC)):
         outg[i] = run.astype(BF)
-        factor = recvf[i, STATE : STATE + 16].astype(F32)
-        run = (factor[0:1] + factor[1:2]) * run + recvg[i].astype(F32)
-    for k in range(1, NC):
-        back(outg, ds_in, rg_send, rg_recv, k).start()
+        if i == NC - 1:
+            run = recvg[i].astype(F32)
+        elif i > 0:
+            factor = recvf[i, STATE : STATE + 16].astype(F32)
+            run = (factor[0:1] + factor[1:2]) * run + recvg[i].astype(F32)
+    give_back(outg, ds_in, rg_send, rg_recv, NC - 1)
     ds_in[seq] = outg[seq]
 
-    lax.fori_loop(NC // 2, NC, intra, 0)
-
-    for k in range(1, NC):
-        from_slab(outf, s_in, rf_send, rf_recv, k).wait_recv()
-        from_slab(outg, ds_in, rg_send, rg_recv, k).wait_recv()
-
-    def to_sibling(k):
+    lax.fori_loop(6, NC, intra, 0)
+
+    def to_sibling(t, k):
         c = chip_at(k)
         return remote(
-            stage.at[c, :, rows_of(1 - core, ROWS)], sib.at[c], sib_send.at[k], sib_recv.at[k], sibling
-        )
-
-    def to_owner(k):
+            stage.at[c, t, rows_of(1 - core, ROWS)],
+            sib.at[c, t],
+            sib_send.at[t, k],
+            sib_recv.at[t, k],
+            sibling,
+        )
+
+    def to_owner(t, k):
         return remote(
-            fin.at[chip_at(k)],
-            gbc.at[:, :, rows_of(chip, STATE)],
-            fin_send.at[k],
-            fin_recv.at[k],
+            fin.at[chip_at(k), t],
+            gbc.at[t, :, rows_of(chip, STATE)],
+            fin_send.at[t, k],
+            fin_recv.at[t, k],
             chip_dev(k),
         )
 
-    def from_group(k):
+    def from_group(t, k):
         return remote(
-            fin.at[chip_at(k)],
-            gbc.at[:, :, rows_of(lax.rem(chip + NC - k, NC), STATE)],
-            fin_send.at[k],
-            fin_recv.at[k],
+            fin.at[chip_at(k), t],
+            gbc.at[t, :, rows_of(chip_back(k), STATE)],
+            fin_send.at[t, k],
+            fin_recv.at[t, k],
             sibling,
         )
 
@@ -369,73 +422,115 @@
             src.at[rows_of(c, L)], dst.at[rows_of(c, L)], out_sem.at[a, c]
         )
 
-    def settle(k):
+    def settle(t, k):
         c = chip_at(k)
-        to_sibling(k).wait_recv()
-        total = (stage[c, :, rows_of(core, ROWS)] + sib[c]).astype(BF)
+        to_sibling(t, k).wait_recv()
+        total = (stage[c, t, rows_of(core, ROWS)] + sib[c, t]).astype(BF)
 
         @pl.when(k == 0)
         def _():
-            gbc[:, :, rows_of(chip, STATE)] = total
+            gbc[t, :, rows_of(chip, STATE)] = total
 
         @pl.when(k > 0)
         def _():
-            fin[c] = total
-            to_owner(k).start()
-
-    def finish(k, carry):
+            fin[c, t] = total
+            to_owner(t, k).start()
+
+    def finish_y(k, carry):
         c = chip_at(k)
         r = rows_of(c, L)
-        b_c, c_c = bc_v[0, r, :], bc_v[1, r, :]
-        d_b, d_c = stage[c, 0], stage[c, 1]
+        c_c = bc_v[1, r, :]
+        d_c = stage[c, 1]
         q = jnp.zeros((H, L), F32)
+        for p in range(W // 256):
+            col = slice(256 * p, 256 * p + 256)
+            start = jnp.concatenate([s_in[2 * p], s_in[2 * p + 1]], axis=1).astype(F32)
+            s_b = (s_loc[c, :, col].astype(F32) + prew[c][:, col] * start).astype(BF)
+            s_loc[c, :, col] = s_b
+            d_c = d_c + nt(dyw[r, col], s_b)
+            y_core = yd[r, col] + ecw[r, col] * nn(c_c, s_b)
+            q = q + by_head(dy[r, col].astype(F32) * y_core, col)
+            x, z, g = (v[r, col].astype(F32) for v in (x_v, z_v, g_v))
+            sig = 1.0 / (1.0 + jnp.exp(-z))
+            silu = z * sig
+            y = y_core + skw[:, col] * x
+            z_v[r, col] = (y * silu).astype(BF)
+            g_v[r, col] = (g * y * (sig + silu * (1.0 - sig))).astype(BF)
+            skipacc[:, col] += jnp.sum((g * silu * x).reshape(L // 8, 8, 256), axis=0)
+        stage[c, 1] = d_c
+        qs[c] = q
+        store(1, c).start()
+        store(2, c).start()
+        to_sibling(1, k).start()
+        return carry
+
+    def finish_b(k, carry):
+        c = chip_at(k)
+        r = rows_of(c, L)
+        d_b = stage[c, 0]
+        for p in range(W // 256):
+            col = slice(256 * p, 256 * p + 256)
+            end = jnp.concatenate([ds_in[2 * p], ds_in[2 * p + 1]], axis=1).astype(F32)
+            ds_b = (ds_loc[c + 1, :, col].astype(F32) + postw[c + 1][:, col] * end).astype(BF)
+            ds_loc[c + 1, :, col] = ds_b
+            d_b = d_b + nt(xw[r, col], ds_b)
+        stage[c, 0] = d_b
+        to_sibling(0, k).start()
+        return carry
+
+    def finish_x(c, carry):
+        r = rows_of(c, L)
+        b_c = bc_v[0, r, :]
         px = jnp.zeros((H, L), F32)
         for p in range(W // 256):
             col = slice(256 * p, 256 * p + 256)
-            start = jnp.concatenate([s_in[2 * p], s_in[2 * p + 1]], axis=1).astype(F32)
-            end = jnp.concatenate([ds_in[2 * p], ds_in[2 * p + 1]], axis=1).astype(F32)
-            s_t = s_loc[c, :, col].astype(F32) + prew[c][:, col] * start
-            ds_t = ds_loc[c + 1, :, col].astype(F32) + postw[c + 1][:, col] * end
-            ds_p = ds_loc[c, :, col].astype(F32) + postw[c][:, col] * end
-            fw[c, :, col] = jnp.sum(s_t * ds_p, axis=0, keepdims=True)
-            s_b, ds_b = s_t.astype(BF), ds_t.astype(BF)
-            d_c = d_c + nt(dyw[r, col], s_b)
-            d_b = d_b + nt(xw[r, col], ds_b)
-            y_core = yd[r, col] + ecw[r, col].astype(F32) * nn(c_c, s_b)
-            dx = dxd[r, col] + ww[r, col].astype(F32) * nn(b_c, ds_b)
-            e_c = e_s[:, col]
-            p_x = xp[r, col].astype(F32) * dx
-            q_x = dy[r, col].astype(F32) * y_core - p_x
-            q_h = q_x.astype(BF)
-            q_l = (q_x - q_h.astype(F32)).astype(BF)
-            q = q + nt(e_c, q_h) + nt(e_c, q_l)
-            px = px + nt(e_c, p_x.astype(BF))
-            x, z, g = (v[r, col].astype(F32) for v in (x_v, z_v, g_v))
-            skip = skw[:, col]
-            sig = 1.0 / (1.0 + jnp.exp(-z))
-            silu = z * sig
-            y = y_core + skip * x
-            dy_f = g * silu
-            z_v[r, col] = (y * silu).astype(BF)
-            g_v[r, col] = (g * y * (sig + silu * (1.0 - sig))).astype(BF)
-            x_v[r, col] = (skip * dy_f + dtw[r, col].astype(F32) * dx).astype(BF)
-            skipacc[:, col] += jnp.sum((dy_f * x).reshape(L // 8, 8, 256), axis=0)
-        stage[c, 0] = d_b
-        stage[c, 1] = d_c
-        qs[c] = q
-        ps[c] = px
-        for a in range(3):
-            store(a, c).start()
-        to_sibling(k).start()
-
-        @pl.when(k > 0)
-        def _():
-            settle(k - 1)
-
+            pair = s_loc[c, :, col].astype(F32) * ds_loc[c, :, col].astype(F32)
+            fw[c, :, col] = jnp.sum(pair, axis=0, keepdims=True)
+            off = ww[r, col] * nn(b_c, ds_loc[c + 1, :, col])
+            px = px + nt(e_s[0:H, col], (xp[r, col].astype(F32) * off).astype(BF))
+            dx = dxd[r, col] + off
+            x_v[r, col] = (skw[:, col] * dy[r, col].astype(F32) + dtw[r, col] * dx).astype(BF)
+        total = ps[c] + px
+        ps[c] = total
+        qs[c] = qs[c] - total
+        store(0, c).start()
         return carry
 
-    lax.fori_loop(0, NC, finish, 0)
-    settle(NC - 1)
+    def settle_all(t):
+        def one(k, carry):
+            settle(t, k)
+            return carry
+
+        lax.fori_loop(0, NC, one, 0)
+
+    @pl.when(seq == 0)
+    def _():
+        s_in[...] = jnp.zeros_like(s_in)
+
+    @pl.when(seq != 0)
+    def _():
+        for k in range(1, NC):
+            from_slab(outf, s_in, rf_send, rf_recv, k).wait_recv()
+
+    lax.fori_loop(0, NC, finish_y, 0)
+    settle_all(1)
+
+    @pl.when(seq == NC - 1)
+    def _():
+        ds_in[...] = jnp.zeros_like(ds_in)
+
+    @pl.when(seq != NC - 1)
+    def _():
+        for k in range(1, NC):
+            from_slab(outg, ds_in, rg_send, rg_recv, k).wait_recv()
+
+    lax.fori_loop(0, NC, finish_b, 0)
+    settle_all(0)
+    for p in range(W // 256):
+        col = slice(256 * p, 256 * p + 256)
+        end = jnp.concatenate([ds_in[2 * p], ds_in[2 * p + 1]], axis=1).astype(F32)
+        ds_loc[0, :, col] = (ds_loc[0, :, col].astype(F32) + postw[0][:, col] * end).astype(BF)
+    lax.fori_loop(0, NC, finish_x, 0)
 
     q = qs[...].reshape(L, L)
     px = ps[...].reshape(L, L)
@@ -443,7 +538,7 @@
     pairs = dot(spread_f, fw[...].reshape(NC, W), 1, 1, HIGHEST)
     boundary = jnp.concatenate([pairs[:, c : c + 1] for c in range(NC)], axis=0)
     d_decay = boundary - before
-    d_step = px / step_r.astype(F32) + rate * d_decay
+    d_step = px / step + rate * d_decay
     d_raw = d_step / (1.0 + jnp.exp(-pre))
     for c in range(NC):
         gdt_ref[:, L * c : L * c + L] = d_raw[H * c : H * c + H].astype(BF)
@@ -469,7 +564,8 @@
     for k in range(1, NC):
         share(k).start()
     for k in range(1, NC):
-        from_group(k).wait_recv()
+        for t in range(2):
+            from_group(t, k).wait_recv()
     outs = [
         pltpu.make_async_copy(gbc.at[0], gb_hbm, gout_sem.at[0]),
         pltpu.make_async_copy(gbc.at[1], gc_hbm, gout_sem.at[1]),
@@ -491,18 +587,47 @@
     for k in range(NC):
         for t in range(2):
             spread(t, k).wait_send()
-        to_sibling(k).wait_send()
+            to_sibling(t, k).wait_send()
     for k in range(1, NC):
-        forward(k, True).wait_send()
-        to_joiner(sendf, recvf, xf_send, xf_recv, k).wait_send()
-        to_joiner(sendg, recvg, xg_send, xg_recv, k).wait_send()
-        back(outf, s_in, rf_send, rf_recv, k).wait_send()
-        back(outg, ds_in, rg_send, rg_recv, k).wait_send()
-        to_owner(k).wait_send()
+        for t in range(2):
+            forward(t, k, True).wait_send()
+            to_owner(t, k).wait_send()
+
+        @pl.when(seq != NC - 1)
+        def _():
+            to_joiner(sendf, recvf, xf_send, xf_recv, k).wait_send()
+
+        @pl.when(seq != 0)
+        def _():
+            to_joiner(sendg, recvg, xg_send, xg_recv, k).wait_send()
+
+        @pl.when(slab_at(k) != 0)
+        def _():
+            back(outf, s_in, rf_send, rf_recv, k).wait_send()
+
+        @pl.when(slab_at(k) != NC - 1)
+        def _():
+            back(outg, ds_in, rg_send, rg_recv, k).wait_send()
+
         share(k).wait_send()
     for c in range(NC):
         for a in range(3):
             store(a, c).wait()
+
+
+def hand_out(*refs):
+    ins, outs, held, (in_sem, out_sem) = refs[:9], refs[9:18], refs[18:27], refs[27:]
+    blocks = [(a, pl.ds(L * c, L), NC * a + c) for c in range(NC) for a in range(3)]
+    blocks += [(a, slice(None), 3 * NC + a - 3) for a in range(3, 9)]
+    loads = [pltpu.make_async_copy(ins[a].at[r], held[a].at[r], in_sem.at[s]) for a, r, s in blocks]
+    stores = [pltpu.make_async_copy(held[a].at[r], outs[a].at[r], out_sem.at[s]) for a, r, s in blocks]
+    for load in loads:
+        load.start()
+    for load, store in zip(loads, stores):
+        load.wait()
+        store.start()
+    for store in stores:
+        store.wait()
 
 
 def per_device(inner_x, gate_z, dt_raw, b_proj, c_proj, a_log, dt_bias, d_skip, grad_gated):
@@ -515,14 +640,15 @@
     rows = jax.ShapeDtypeStruct((ROWS, GROUPS * STATE), BF)
     head = jax.ShapeDtypeStruct((1, H), F32)
     wide = pltpu.VMEM((tokens, W), BF)
+    wide_f = pltpu.VMEM((tokens, W), F32)
     scratch = [
         wide, wide, wide,
         wide, wide, wide, wide,
-        wide, wide, wide,
-        pltpu.VMEM((H, W), BF),
-        pltpu.VMEM((NC, L, H), BF),
-        pltpu.VMEM((NC, L, H), BF),
-        pltpu.VMEM((NC, L, H), BF),
+        wide_f, wide_f, wide_f,
+        pltpu.VMEM((2 * H, W), BF),
+        pltpu.VMEM((NC, L, 2 * H), BF),
+        pltpu.VMEM((NC, L, 2 * H), BF),
+        pltpu.VMEM((NC, L, 2 * H), BF),
         pltpu.VMEM((NC, H, L), F32),
         pltpu.VMEM((NC, L, H), F32),
         pltpu.VMEM((NC, 1, W), F32),
@@ -553,15 +679,16 @@
         pltpu.VMEM((NC, H, L), F32),
         pltpu.VMEM((NC, H, L), F32),
         sem((3, NC)), sem((3, NC)), sem((2,)),
-        sem((2, NC)), sem((2, NC)), sem((NC,)), sem((NC,)),
+        sem((2, NC)), sem((2, NC)), sem((2, NC)), sem((2, NC)),
         sem((NC,)), sem((NC,)), sem((NC,)), sem((NC,)),
         sem((NC,)), sem((NC,)), sem((NC,)), sem((NC,)),
-        sem((NC,)), sem((NC,)), sem((NC,)), sem((NC,)), sem((NC,)), sem((NC,)),
+        sem((2, NC)), sem((2, NC)), sem((2, NC)), sem((2, NC)), sem((NC,)), sem((NC,)),
         sem((2,)),
     ]
+    small = (jax.ShapeDtypeStruct((H, tokens), BF), rows, rows, head, head, head)
     outs = pl.pallas_call(
         kernel,
-        out_shape=(big, big, big, jax.ShapeDtypeStruct((H, tokens), BF), rows, rows, head, head, head),
+        out_shape=(big, big, big) + small,
         in_specs=[any_space, any_space, any_space, vmem, any_space, any_space, smem, smem, smem],
         out_specs=(any_space, any_space, any_space, vmem, any_space, any_space, vmem, vmem, vmem),
         scratch_shapes=scratch,
@@ -569,11 +696,16 @@
             collective_id=0, has_side_effects=True, vmem_limit_bytes=60 * 2**20
         ),
     )(inner_x, gate_z, grad_gated, dt_raw, b_proj, c_proj, a_log, dt_bias, d_skip)
-    gated, grad_x, grad_z, grad_dt, grad_b, grad_c, g_alog, g_bias, g_skip = outs
-    return (
-        gated, grad_x, grad_z, grad_dt, grad_b, grad_c,
-        g_alog.reshape(H), g_bias.reshape(H), g_skip.reshape(H),
-    )
+    outs = pl.pallas_call(
+        hand_out,
+        out_shape=(big, big, big) + small,
+        in_specs=[any_space] * 9,
+        out_specs=(any_space,) * 9,
+        scratch_shapes=[pltpu.VMEM(v.shape, v.dtype) for v in outs]
+        + [sem((3 * NC + 6,)), sem((3 * NC + 6,))],
+        compiler_params=pltpu.CompilerParams(vmem_limit_bytes=60 * 2**20),
+    )(*outs)
+    return outs[:6] + tuple(v.reshape(H) for v in outs[6:])
 
 
 def solution(mesh):

time: 81.1 us -> 71.8 us (0.89)
  local copies, waits for them, and re-layouts: 10.5 us -> 0 us
  Pallas kernels: 69 us -> 71 us
    unnamed x25 -> x0, local copies, waits for them, and re-layouts: 10.5 us -> none
    pallas_call x1 -> x2, Pallas kernels: 69 us -> 71 us  [the longest x1 65.1 us: per_device(): pl.pallas_call(kernel, out_shape=(big, big, big) + small, in_specs=[any_s...]
where the time goes in v2:
time: 71.8 us; the launch traced here: 71.6 us
  Pallas kernels  71 us (99%)
    pallas_call x1, Pallas kernels, per_device(): pl.pallas_call(kernel, out_shape=(big, big, big) + small, in_specs=[any_s...  65.1 us
    pallas_call x1, Pallas kernels, per_device(): pl.pallas_call(hand_out, out_shape=(big, big, big) + small, in_specs=[any...  5.91 us

profile of v2, /device:TPU:1, one launch (start us, length us, event | category | flops | bytes accessed | tf_op | source)
XLA Modules:
  0.0 71.6 jit_solution(17996794710244298996)
XLA Ops:
  0.6 65.1 %shard_map.160 = (bf16[1024,1024]{1,0:T(8,128)(2,1)}, bf16[1024,1024]{1,0:T(8,128)(2,1)}, bf16[1024,1024]{1,0:T(8,128)(2,1)}, bf16[16,1024]{1,0:T(8,128)(2,1)}, ...) custom-call(bf16[1024,1024]{1,0:T(8,128)(2,1)} %x_hbm.1, ...), custom_call_target="tpu_custom_call" | custom-call | tf_op jit(solution)/shard_map/pallas_call | solution.py:689
  65.7 5.9 %shard_map.161 = (bf16[1024,1024]{1,0:T(8,128)(2,1)}, bf16[1024,1024]{1,0:T(8,128)(2,1)}, bf16[1024,1024]{1,0:T(8,128)(2,1)}, bf16[16,1024]{1,0:T(8,128)(2,1)}, ...) custom-call(bf16[1024,1024]{1,0:T(8,128)(2,1)} %get-tuple-element.27, ...), custom_call_target="tpu_custom_call" | custom-call | tf_op jit(solution)/shard_map/pallas_call | solution.py:699

commit v3 on v2

--- a/solution.py
+++ b/solution.py
@@ -47,6 +47,15 @@
         device_id=device,
         device_id_type=MESH,
     )
+
+
+def repeat(first, last, body, times):
+    def some(i, carry):
+        for j in range(times):
+            body(first + i * times + j, carry)
+        return carry
+
+    lax.fori_loop(0, (last - first) // times, some, 0)
 
 
 def rows_of(index, count):
@@ -110,49 +119,6 @@
         pl.semaphore_signal(barrier, inc=1, device_id=chip_dev(k), device_id_type=MESH)
         pl.semaphore_signal(barrier, inc=1, device_id=slab_dev(k), device_id_type=MESH)
     pl.semaphore_signal(barrier, inc=1, device_id=sibling, device_id_type=MESH)
-    pl.semaphore_wait(barrier, 2 * NC - 1)
-
-    def spread(t, k):
-        src = (b_hbm, c_hbm)[t]
-        device = sibling if k == 0 else chip_dev(k)
-        group = chip if k == 0 else chip_at(k)
-        return remote(
-            src.at[:, rows_of(group, STATE)],
-            bc_v.at[t, rows_of(hd, ROWS)],
-            a_send.at[t, k],
-            a_recv.at[t, k],
-            device,
-        )
-
-    def arrived(t, k):
-        place = 2 * chip + 1 - core if k == 0 else 2 * chip_back(k) + core
-        return remote(
-            b_hbm.at[:, rows_of(chip, STATE)],
-            bc_v.at[t, rows_of(place, ROWS)],
-            a_send.at[t, k],
-            a_recv.at[t, k],
-            sibling,
-        )
-
-    def forward(t, k, mine):
-        place = 2 * chip_back(k) + (core if mine else 1 - core)
-        block = bc_v.at[t, rows_of(place, ROWS)]
-        return remote(block, block, f_send.at[t, k], f_recv.at[t, k], sibling)
-
-    for t in range(2):
-        for k in (6, 5, 7, 4, 2, 1, 3, 0):
-            spread(t, k).start()
-
-    def pass_on(t):
-        for k in (4, 1, 3, 2, 5, 7, 6):
-            arrived(t, k).wait_recv()
-            forward(t, k, True).start()
-
-    def complete(t):
-        own_bc(t).wait()
-        arrived(t, 0).wait_recv()
-        for k in range(1, NC):
-            forward(t, k, False).wait_recv()
 
     row16 = lax.broadcasted_iota(jnp.int32, (H, L), 0)
 
@@ -208,6 +174,50 @@
     postw[0] = run
     skipacc[...] = jnp.zeros_like(skipacc)
 
+    pl.semaphore_wait(barrier, 2 * NC - 1)
+
+    def spread(t, k):
+        src = (b_hbm, c_hbm)[t]
+        device = sibling if k == 0 else chip_dev(k)
+        group = chip if k == 0 else chip_at(k)
+        return remote(
+            src.at[:, rows_of(group, STATE)],
+            bc_v.at[t, rows_of(hd, ROWS)],
+            a_send.at[t, k],
+            a_recv.at[t, k],
+            device,
+        )
+
+    def arrived(t, k):
+        place = 2 * chip + 1 - core if k == 0 else 2 * chip_back(k) + core
+        return remote(
+            b_hbm.at[:, rows_of(chip, STATE)],
+            bc_v.at[t, rows_of(place, ROWS)],
+            a_send.at[t, k],
+            a_recv.at[t, k],
+            sibling,
+        )
+
+    def forward(t, k, mine):
+        place = 2 * chip_back(k) + (core if mine else 1 - core)
+        block = bc_v.at[t, rows_of(place, ROWS)]
+        return remote(block, block, f_send.at[t, k], f_recv.at[t, k], sibling)
+
+    for t in range(2):
+        for k in (6, 5, 7, 4, 2, 1, 3, 0):
+            spread(t, k).start()
+
+    def pass_on(t):
+        for k in (4, 1, 3, 2, 5, 7, 6):
+            arrived(t, k).wait_recv()
+            forward(t, k, True).start()
+
+    def complete(t):
+        own_bc(t).wait()
+        arrived(t, 0).wait_recv()
+        for k in range(1, NC):
+            forward(t, k, False).wait_recv()
+
     def prepare_x(c, carry):
         load(0, c).wait()
         r = rows_of(c, L)
@@ -232,14 +242,21 @@
             col = slice(256 * p, 256 * p + 256)
             ec_w = nn(ec_c, e_s[:, col])
             ecw[r, col] = ec_w
-            z = z_v[r, col].astype(F32)
-            dy_f = g_v[r, col].astype(F32) * (z / (1.0 + jnp.exp(-z)))
+            x, z, g = (v[r, col].astype(F32) for v in (x_v, z_v, g_v))
+            sig = 1.0 / (1.0 + jnp.exp(-z))
+            silu = z * sig
+            dy_f = g * silu
             dy[r, col] = dy_f.astype(BF)
             dyw[r, col] = (dy_f * ec_w).astype(BF)
+            z_v[r, col] = silu.astype(BF)
+            g_v[r, col] = (g * (sig + silu * (1.0 - sig))).astype(BF)
+            skipacc[:, col] += jnp.sum((dy_f * x).reshape(L // 8, 8, 256), axis=0)
         return carry
 
-    lax.fori_loop(0, NC, prepare_x, 0)
+    repeat(0, NC, prepare_x, 2)
+    repeat(0, NC // 2, prepare_g, 2)
     pass_on(0)
+    repeat(NC // 2, NC, prepare_g, 2)
     complete(0)
 
     def scan_state(first, keep, t, source, order):
@@ -256,7 +273,7 @@
                 s_acc[:, col] = elw[c][:, col] * now + nn(rows_t, source[r, col])
             return carry
 
-        lax.fori_loop(0, NC, one, 0)
+        repeat(0, NC, one, 4)
 
     def to_joiner(src, dst, send_sem, recv_sem, k):
         return remote(src.at[slab_at(k)], dst.at[seq], send_sem.at[k], recv_sem.at[k], slab_dev(k))
@@ -282,7 +299,7 @@
     recvf[seq] = sendf[seq]
 
     pass_on(1)
-    lax.fori_loop(0, NC, prepare_g, 0)
+    skip_sum = jnp.sum(dot(spread_f, skipacc[...], 1, 1, HIGHEST), axis=1, keepdims=True)
     complete(1)
     scan_state(1, ds_loc, 1, dyw, lambda i: NC - 1 - i)
     for p in range(W // 256):
@@ -307,13 +324,16 @@
         high = v.astype(BF)
         low_part = (v - high.astype(F32)).astype(BF)
         e_c = e_s[0:H, col]
-        return nt(e_c, high) + nt(e_c, low_part)
+        return nt(
+            jnp.concatenate([e_c, e_c], axis=1), jnp.concatenate([high, low_part], axis=1)
+        )
 
     def intra(c, carry):
         r = rows_of(c, L)
         b_c, c_c = bc_v[0, r, :], bc_v[1, r, :]
         scores = jnp.where(low, nt(c_c, b_c), 0.0)
         d_scores = jnp.zeros((L, L), F32)
+        q = jnp.zeros((H, L), F32)
         px = jnp.zeros((H, L), F32)
         cum_r, cum_c = cumv[c], cumt[c]
         for p in range(H // 2):
@@ -329,18 +349,26 @@
                 parts.append((scores * mask).astype(BF))
                 d_scores = d_scores + d_mix[:, L * j : L * j + L] * mask
             mix = jnp.concatenate(parts, axis=1)
-            yd[r, col] = nn(mix, x_two)
-            both = tn(mix, dy_p)
-            dx = jnp.where(left > 0.0, both[:L], both[L:])
+            y = nn(mix, x_two)
+            yd[r, col] = y
+            mix_t = jnp.concatenate([jnp.transpose(v) for v in parts], axis=1)
+            dx = nn(mix_t, jnp.concatenate([dy_p * left_b, dy_p * right_b], axis=0))
             dxd[r, col] = dx
-            px = px + by_head(x_p.astype(F32) * dx, col)
+            p_x = x_p.astype(F32) * dx
+            q = q + by_head(dy_p.astype(F32) * y - p_x, col)
+            px = px + nt(e_s[0:H, col], p_x.astype(BF))
         d_scores = jnp.where(low, d_scores, 0.0).astype(BF)
-        stage[c, 0] = tn(d_scores, c_c)
+        d_b = tn(d_scores, c_c)
+        for p in range(W // 256):
+            col = slice(256 * p, 256 * p + 256)
+            d_b = d_b + nt(xw[r, col], ds_loc[c + 1, :, col])
+        stage[c, 0] = d_b
         stage[c, 1] = nn(d_scores, b_c)
+        qs[c] = q
         ps[c] = px
         return carry
 
-    lax.fori_loop(0, 3, intra, 0)
+    repeat(0, 2, intra, 2)
 
     def collect(src, dst, send_sem, recv_sem, absent):
         for k in range(1, NC):
@@ -373,7 +401,7 @@
 
     give_back(outf, s_in, rf_send, rf_recv, 0)
     s_in[seq] = outf[seq]
-    lax.fori_loop(3, 6, intra, 0)
+    repeat(2, 6, intra, 2)
     collect(sendg, recvg, xg_send, xg_recv, 0)
     run = jnp.zeros((STATE, L), F32)
     for i in reversed(range(NC)):
@@ -386,15 +414,14 @@
     give_back(outg, ds_in, rg_send, rg_recv, NC - 1)
     ds_in[seq] = outg[seq]
 
-    lax.fori_loop(6, NC, intra, 0)
-
-    def to_sibling(t, k):
-        c = chip_at(k)
+    repeat(6, NC, intra, 2)
+
+    def to_sibling(t, c):
         return remote(
             stage.at[c, t, rows_of(1 - core, ROWS)],
             sib.at[c, t],
-            sib_send.at[t, k],
-            sib_recv.at[t, k],
+            sib_send.at[t, c],
+            sib_recv.at[t, c],
             sibling,
         )
 
@@ -424,7 +451,7 @@
 
     def settle(t, k):
         c = chip_at(k)
-        to_sibling(t, k).wait_recv()
+        to_sibling(t, c).wait_recv()
         total = (stage[c, t, rows_of(core, ROWS)] + sib[c, t]).astype(BF)
 
         @pl.when(k == 0)
@@ -442,41 +469,59 @@
         c_c = bc_v[1, r, :]
         d_c = stage[c, 1]
         q = jnp.zeros((H, L), F32)
-        for p in range(W // 256):
+
+        def states(p):
             col = slice(256 * p, 256 * p + 256)
             start = jnp.concatenate([s_in[2 * p], s_in[2 * p + 1]], axis=1).astype(F32)
             s_b = (s_loc[c, :, col].astype(F32) + prew[c][:, col] * start).astype(BF)
             s_loc[c, :, col] = s_b
-            d_c = d_c + nt(dyw[r, col], s_b)
-            y_core = yd[r, col] + ecw[r, col] * nn(c_c, s_b)
-            q = q + by_head(dy[r, col].astype(F32) * y_core, col)
-            x, z, g = (v[r, col].astype(F32) for v in (x_v, z_v, g_v))
-            sig = 1.0 / (1.0 + jnp.exp(-z))
-            silu = z * sig
-            y = y_core + skw[:, col] * x
-            z_v[r, col] = (y * silu).astype(BF)
-            g_v[r, col] = (g * y * (sig + silu * (1.0 - sig))).astype(BF)
-            skipacc[:, col] += jnp.sum((g * silu * x).reshape(L // 8, 8, 256), axis=0)
+            return nt(dyw[r, col], s_b), nn(c_c, s_b)
+
+        ahead = states(0)
+        for p in range(W // 256):
+            col = slice(256 * p, 256 * p + 256)
+            now = ahead
+            if p + 1 < W // 256:
+                ahead = states(p + 1)
+            d_c = d_c + now[0]
+            off = ecw[r, col] * now[1]
+            q = q + nt(e_s[0:H, col], (dy[r, col].astype(F32) * off).astype(BF))
+            y = yd[r, col] + off + skw[:, col] * x_v[r, col].astype(F32)
+            z_v[r, col] = (y * z_v[r, col].astype(F32)).astype(BF)
+            g_v[r, col] = (y * g_v[r, col].astype(F32)).astype(BF)
         stage[c, 1] = d_c
-        qs[c] = q
+        qs[c] += q
         store(1, c).start()
         store(2, c).start()
-        to_sibling(1, k).start()
+        to_sibling(1, c).start()
+
+        @pl.when(k >= 2)
+        def _():
+            settle(1, k - 2)
+
         return carry
 
-    def finish_b(k, carry):
-        c = chip_at(k)
-        r = rows_of(c, L)
-        d_b = stage[c, 0]
+    def two(p):
+        return jnp.concatenate([ds_in[2 * p], ds_in[2 * p + 1]], axis=1)
+
+    def finish_b(m, carry):
+        d_b = jnp.zeros((2 * L, STATE), F32)
         for p in range(W // 256):
             col = slice(256 * p, 256 * p + 256)
-            end = jnp.concatenate([ds_in[2 * p], ds_in[2 * p + 1]], axis=1).astype(F32)
-            ds_b = (ds_loc[c + 1, :, col].astype(F32) + postw[c + 1][:, col] * end).astype(BF)
-            ds_loc[c + 1, :, col] = ds_b
-            d_b = d_b + nt(xw[r, col], ds_b)
-        stage[c, 0] = d_b
-        to_sibling(0, k).start()
+            scaled = [
+                (xw[rows_of(c, L), col].astype(F32) * postw[c + 1][:, col]).astype(BF)
+                for c in (2 * m, 2 * m + 1)
+            ]
+            d_b = d_b + nt(jnp.concatenate(scaled, axis=0), two(p))
+        for j in range(2):
+            stage[2 * m + j, 0] += d_b[L * j : L * j + L]
+            to_sibling(0, 2 * m + j).start()
         return carry
+
+    def whole(c, p):
+        col = slice(256 * p, 256 * p + 256)
+        ds_t = ds_loc[c, :, col].astype(F32) + postw[c][:, col] * two(p).astype(F32)
+        ds_loc[c, :, col] = ds_t.astype(BF)
 
     def finish_x(c, carry):
         r = rows_of(c, L)
@@ -484,24 +529,24 @@
         px = jnp.zeros((H, L), F32)
         for p in range(W // 256):
             col = slice(256 * p, 256 * p + 256)
-            pair = s_loc[c, :, col].astype(F32) * ds_loc[c, :, col].astype(F32)
-            fw[c, :, col] = jnp.sum(pair, axis=0, keepdims=True)
+            whole(c + 1, p)
             off = ww[r, col] * nn(b_c, ds_loc[c + 1, :, col])
             px = px + nt(e_s[0:H, col], (xp[r, col].astype(F32) * off).astype(BF))
             dx = dxd[r, col] + off
             x_v[r, col] = (skw[:, col] * dy[r, col].astype(F32) + dtw[r, col] * dx).astype(BF)
-        total = ps[c] + px
-        ps[c] = total
-        qs[c] = qs[c] - total
+            pair = s_loc[c, :, col].astype(F32) * ds_loc[c, :, col].astype(F32)
+            fw[c, :, col] = jnp.sum(pair, axis=0, keepdims=True)
+        ps[c] += px
+        qs[c] -= px
         store(0, c).start()
         return carry
 
-    def settle_all(t):
+    def settle_from(t, first):
         def one(k, carry):
             settle(t, k)
             return carry
 
-        lax.fori_loop(0, NC, one, 0)
+        lax.fori_loop(first, NC, one, 0)
 
     @pl.when(seq == 0)
     def _():
@@ -512,8 +557,8 @@
         for k in range(1, NC):
             from_slab(outf, s_in, rf_send, rf_recv, k).wait_recv()
 
-    lax.fori_loop(0, NC, finish_y, 0)
-    settle_all(1)
+    repeat(0, NC, finish_y, 2)
+    settle_from(1, NC - 2)
 
     @pl.when(seq == NC - 1)
     def _():
@@ -524,13 +569,12 @@
         for k in range(1, NC):
             from_slab(outg, ds_in, rg_send, rg_recv, k).wait_recv()
 
-    lax.fori_loop(0, NC, finish_b, 0)
-    settle_all(0)
+    lax.fori_loop(0, NC // 2, finish_b, 0)
     for p in range(W // 256):
-        col = slice(256 * p, 256 * p + 256)
-        end = jnp.concatenate([ds_in[2 * p], ds_in[2 * p + 1]], axis=1).astype(F32)
-        ds_loc[0, :, col] = (ds_loc[0, :, col].astype(F32) + postw[0][:, col] * end).astype(BF)
-    lax.fori_loop(0, NC, finish_x, 0)
+        whole(0, p)
+    repeat(0, 2, finish_x, 2)
+    settle_from(0, 0)
+    repeat(2, NC, finish_x, 2)
 
     q = qs[...].reshape(L, L)
     px = ps[...].reshape(L, L)
@@ -550,7 +594,6 @@
             total = total + column[H * c : H * c + H]
         return total
 
-    skip_sum = jnp.sum(dot(spread_f, skipacc[...], 1, 1, HIGHEST), axis=1, keepdims=True)
     lane16 = lax.broadcasted_iota(jnp.int32, (H, L), 1)
     par[0] = jnp.where(
         lane16 == 0,

time: 71.8 us -> 69.1 us (0.962)
  Pallas kernels: 71 us -> 68.1 us
    pallas_call x1, Pallas kernels: 65.1 us -> 62.1 us  [per_device(): pl.pallas_call(kernel, out_shape=(big, big, big) + small, in_specs=[any_s...]
where the time goes in v3:
time: 69.1 us; the launch traced here: 68.9 us
  Pallas kernels  68.1 us (99%)
  between operations  0.81 us (1%)
    pallas_call x1, Pallas kernels, per_device(): pl.pallas_call(kernel, out_shape=(big, big, big) + small, in_specs=[any_s...  62.1 us
    pallas_call x1, Pallas kernels, per_device(): pl.pallas_call(hand_out, out_shape=(big, big, big) + small, in_specs=[any...  5.91 us

profile of v3, /device:TPU:1, one launch (start us, length us, event | category | flops | bytes accessed | tf_op | source)
XLA Modules:
  0.0 68.9 jit_solution(15496485521254045142)
XLA Ops:
  0.6 62.1 %shard_map.160 = (bf16[1024,1024]{1,0:T(8,128)(2,1)}, bf16[1024,1024]{1,0:T(8,128)(2,1)}, bf16[1024,1024]{1,0:T(8,128)(2,1)}, bf16[16,1024]{1,0:T(8,128)(2,1)}, ...) custom-call(bf16[1024,1024]{1,0:T(8,128)(2,1)} %x_hbm.1, ...), custom_call_target="tpu_custom_call" | custom-call | tf_op jit(solution)/shard_map/pallas_call | solution.py:732
  62.8 5.9 %shard_map.161 = (bf16[1024,1024]{1,0:T(8,128)(2,1)}, bf16[1024,1024]{1,0:T(8,128)(2,1)}, bf16[1024,1024]{1,0:T(8,128)(2,1)}, bf16[16,1024]{1,0:T(8,128)(2,1)}, ...) custom-call(bf16[1024,1024]{1,0:T(8,128)(2,1)} %get-tuple-element.27, ...), custom_call_target="tpu_custom_call" | custom-call | tf_op jit(solution)/shard_map/pallas_call | solution.py:742

commit v4 on v3

--- a/solution.py
+++ b/solution.py
@@ -109,10 +109,7 @@
         )
 
     for c in range(NC):
-        for a in range(3):
-            load(a, c).start()
-    for t in range(2):
-        own_bc(t).start()
+        load(0, c).start()
 
     barrier = pltpu.get_barrier_semaphore()
     for k in range(1, NC):
@@ -206,6 +203,10 @@
     for t in range(2):
         for k in (6, 5, 7, 4, 2, 1, 3, 0):
             spread(t, k).start()
+        own_bc(t).start()
+    for c in range(NC):
+        load(1, c).start()
+        load(2, c).start()
 
     def pass_on(t):
         for k in (4, 1, 3, 2, 5, 7, 6):
@@ -254,9 +255,7 @@
         return carry
 
     repeat(0, NC, prepare_x, 2)
-    repeat(0, NC // 2, prepare_g, 2)
     pass_on(0)
-    repeat(NC // 2, NC, prepare_g, 2)
     complete(0)
 
     def scan_state(first, keep, t, source, order):
@@ -299,6 +298,7 @@
     recvf[seq] = sendf[seq]
 
     pass_on(1)
+    repeat(0, NC, prepare_g, 2)
     skip_sum = jnp.sum(dot(spread_f, skipacc[...], 1, 1, HIGHEST), axis=1, keepdims=True)
     complete(1)
     scan_state(1, ds_loc, 1, dyw, lambda i: NC - 1 - i)
@@ -401,7 +401,7 @@
 
     give_back(outf, s_in, rf_send, rf_recv, 0)
     s_in[seq] = outf[seq]
-    repeat(2, 6, intra, 2)
+    repeat(2, 6, intra, 4)
     collect(sendg, recvg, xg_send, xg_recv, 0)
     run = jnp.zeros((STATE, L), F32)
     for i in reversed(range(NC)):
@@ -532,12 +532,19 @@
             whole(c + 1, p)
             off = ww[r, col] * nn(b_c, ds_loc[c + 1, :, col])
             px = px + nt(e_s[0:H, col], (xp[r, col].astype(F32) * off).astype(BF))
-            dx = dxd[r, col] + off
-            x_v[r, col] = (skw[:, col] * dy[r, col].astype(F32) + dtw[r, col] * dx).astype(BF)
+            dxd[r, col] += off
             pair = s_loc[c, :, col].astype(F32) * ds_loc[c, :, col].astype(F32)
             fw[c, :, col] = jnp.sum(pair, axis=0, keepdims=True)
         ps[c] += px
         qs[c] -= px
+        return carry
+
+    def finish_gx(c, carry):
+        r = rows_of(c, L)
+        for p in range(W // 256):
+            col = slice(256 * p, 256 * p + 256)
+            skip = skw[:, col] * dy[r, col].astype(F32)
+            x_v[r, col] = (skip + dtw[r, col] * dxd[r, col]).astype(BF)
         store(0, c).start()
         return carry
 
@@ -557,7 +564,7 @@
         for k in range(1, NC):
             from_slab(outf, s_in, rf_send, rf_recv, k).wait_recv()
 
-    repeat(0, NC, finish_y, 2)
+    repeat(0, NC, finish_y, 4)
     settle_from(1, NC - 2)
 
     @pl.when(seq == NC - 1)
@@ -606,6 +613,7 @@
 
     for k in range(1, NC):
         share(k).start()
+    repeat(0, NC, finish_gx, 2)
     for k in range(1, NC):
         for t in range(2):
             from_group(t, k).wait_recv()

time: 69.1 us -> 68.5 us (level)
  Pallas kernels: 68.1 us -> 67.4 us
where the time goes in v4:
time: 68.5 us; the launch traced here: 68.3 us
  Pallas kernels  67.4 us (98%)
  between operations  0.83 us (1%)
    pallas_call x1, Pallas kernels, per_device(): pl.pallas_call(kernel, out_shape=(big, big, big) + small, in_specs=[any_s...  61.5 us
    pallas_call x1, Pallas kernels, per_device(): pl.pallas_call(hand_out, out_shape=(big, big, big) + small, in_specs=[any...  5.91 us

profile of v4, /device:TPU:1, one launch (start us, length us, event | category | flops | bytes accessed | tf_op | source)
XLA Modules:
  0.0 68.3 jit_solution(13093536620790056049)
XLA Ops:
  0.6 61.5 %shard_map.160 = (bf16[1024,1024]{1,0:T(8,128)(2,1)}, bf16[1024,1024]{1,0:T(8,128)(2,1)}, bf16[1024,1024]{1,0:T(8,128)(2,1)}, bf16[16,1024]{1,0:T(8,128)(2,1)}, ...) custom-call(bf16[1024,1024]{1,0:T(8,128)(2,1)} %x_hbm.1, ...), custom_call_target="tpu_custom_call" | custom-call | tf_op jit(solution)/shard_map/pallas_call | solution.py:740
  62.2 5.9 %shard_map.161 = (bf16[1024,1024]{1,0:T(8,128)(2,1)}, bf16[1024,1024]{1,0:T(8,128)(2,1)}, bf16[1024,1024]{1,0:T(8,128)(2,1)}, bf16[16,1024]{1,0:T(8,128)(2,1)}, ...) custom-call(bf16[1024,1024]{1,0:T(8,128)(2,1)} %get-tuple-element.27, ...), custom_call_target="tpu_custom_call" | custom-call | tf_op jit(solution)/shard_map/pallas_call | solution.py:750
